TPU v7x, 128 devices: a whole 4x4x4 slice. The times are simulated.
128 devices in a mesh: tile: 64 (over y, z_hi, x, core), ch: 2 (over z_lo).
Axes of the slice: x: 4, y: 4, z: 4 (z_hi: 2, z_lo: 2; z = z_hi * 2 + z_lo), core: 2. Of those that a mesh axis runs over, the one named last changes fastest.
Arguments:
- features: bfloat16 [256, 32, 32, 256], P('tile'), may hold values from -6 to 6
- cotangent: bfloat16 [256, 32, 32, 512], P('tile'), may hold values from -6 to 6
- neighbours: int32 [256, 8], P('tile'), may hold values from 0 to 256, as said below
- first_weight: bfloat16 [256, 128], replicated, may hold values from -0.375 to 0.375
- first_bias: float32 [128], replicated, may hold values from -3 to 3
- mid_weight: bfloat16 [3, 3, 128, 128], P(None, None, None, 'ch'), may hold values from -0.1875 to 0.1875
- mid_bias: float32 [128], replicated, may hold values from -3 to 3
- last_weight: bfloat16 [128, 512], P('ch'), may hold values from -0.5 to 0.5
- side_weight: bfloat16 [256, 512], P('ch'), may hold values from -0.375 to 0.375
- last_bias: float32 [512], replicated, may hold values from -3 to 3
Outputs:
- output: bfloat16 [256, 32, 32, 512], P('tile')
- grad_first: float32 [256, 128], P(None, 'ch')
- grad_first_bias: float32 [128], P('ch')
- grad_mid: float32 [3, 3, 128, 128], P(None, None, None, 'ch')
- grad_mid_bias: float32 [128], P('ch')
- grad_last: float32 [128, 512], P('ch')
- grad_side: float32 [256, 512], P('ch')
- grad_last_bias: float32 [512], replicated
Inputs may be any that keep to these rules, and one draw needn't show every extreme that they name: `neighbours`: each tissue tile sits at its own position of a window of 16 x 32 tile positions; row t lists the tiles at the positions up-left, up, up-right, left, right, down-left, down, down-right of tile t, or 256 where that position lies outside the window or holds no tissue. The relation is mutual: if u is t's neighbour in a direction, t is u's neighbour in the opposite direction.
All inputs are finite; a program needn't handle non-finite values.
Results may differ from a plain program's by a relative error of at most 0.018.
Values may be sent and summed in bfloat16 or wider, within the bound.
A program may use at most 128 MiB of HBM per device.

v0:
```python
import math

import jax
import jax.numpy as jnp
from jax import lax
from jax.sharding import PartitionSpec as P

FORWARD_OFFSETS = ((0, 0), (0, 1), (0, 2), (1, 0), (1, 1), (1, 2), (2, 0), (2, 1), (2, 2))
BACKWARD_OFFSETS = ((2, 2), (2, 1), (2, 0), (1, 2), (1, 1), (1, 0), (0, 2), (0, 1), (0, 0))


def silu_slope(values):
    sigma = jax.nn.sigmoid(values)
    return sigma * (1.0 + values * (1.0 - sigma))


def edge_table(tiles_in):
    return jnp.stack(
        [tiles_in[:, 0], tiles_in[:, -1], tiles_in[:, :, 0], tiles_in[:, :, -1]], axis=1
    )


def assemble(tiles_in, strip_table, neighbours):
    table_size = strip_table.shape[0]

    def choose_strip(direction, strip_id):
        owner_ids = neighbours[:, direction]
        present = owner_ids < table_size
        strips = strip_table[jnp.minimum(owner_ids, table_size - 1), strip_id]
        return jnp.where(present[:, None, None], strips, jnp.zeros_like(strips))

    above_row = choose_strip(1, 1)
    below_row = choose_strip(6, 0)
    left_col = choose_strip(3, 3)
    right_col = choose_strip(4, 2)
    up_left = choose_strip(0, 1)[:, -1:]
    up_right = choose_strip(2, 1)[:, :1]
    down_left = choose_strip(5, 0)[:, -1:]
    down_right = choose_strip(7, 0)[:, :1]
    top_band = jnp.concatenate([up_left, above_row, up_right], axis=1)
    bottom_band = jnp.concatenate([down_left, below_row, down_right], axis=1)
    middle = jnp.concatenate([left_col[:, :, None], tiles_in, right_col[:, :, None]], axis=2)
    return jnp.concatenate([top_band[:, None], middle, bottom_band[:, None]], axis=1)


def patch_cols(padded_in, offset_list):
    extent = padded_in.shape[1] - 2
    return jnp.concatenate(
        [
            padded_in[:, row_off : row_off + extent, col_off : col_off + extent, :]
            for row_off, col_off in offset_list
        ],
        axis=-1,
    )


def matmul_rows(left_mat, right_mat):
    return lax.dot_general(
        left_mat, right_mat, (((0,), (0,)), ((), ())), preferred_element_type=jnp.float32
    )


def per_device(
    features,
    cotangent,
    neighbours,
    first_weight,
    first_bias,
    mid_weight,
    mid_bias,
    last_weight,
    side_weight,
    last_bias,
):
    tile_count = features.shape[0]
    extent = features.shape[1]
    in_full = features.shape[3]
    full_mid = mid_weight.shape[2]
    half_mid = mid_weight.shape[3]
    half_in = side_weight.shape[0]
    out_width = last_weight.shape[1]
    tile_devices = lax.axis_size("tile")
    all_tiles = tile_count * tile_devices
    scale_loss = 1.0 / math.sqrt(tile_count * extent * extent)
    group_index = lax.axis_index("ch")
    pixels = tile_count * extent * extent
    flat_in = features.reshape(pixels, in_full)
    first_pre = jnp.dot(flat_in, first_weight, preferred_element_type=jnp.float32) + first_bias
    first_act = (
        jax.nn.silu(first_pre).astype(jnp.bfloat16).reshape(tile_count, extent, extent, full_mid)
    )
    strips_out = edge_table(first_act).reshape(tile_count, 4, extent * full_mid)
    strip_all = lax.all_gather(strips_out, "tile", axis=0, tiled=True)
    strip_all = strip_all.reshape(all_tiles, 4, extent, full_mid)
    padded = assemble(first_act, strip_all, neighbours)
    mid_patches = patch_cols(padded, FORWARD_OFFSETS).reshape(pixels, 9 * full_mid)
    own_mid_bias = lax.dynamic_slice_in_dim(mid_bias, group_index * half_mid, half_mid, 0)
    mid_pre = (
        jnp.dot(
            mid_patches,
            mid_weight.reshape(9 * full_mid, half_mid),
            preferred_element_type=jnp.float32,
        )
        + own_mid_bias
    )
    mid_act = jax.nn.silu(mid_pre).astype(jnp.bfloat16)
    own_in = lax.dynamic_slice_in_dim(flat_in, group_index * half_in, half_in, 1)
    partial_value = jnp.dot(mid_act, last_weight, preferred_element_type=jnp.float32)
    partial_value = partial_value + jnp.dot(own_in, side_weight, preferred_element_type=jnp.float32)
    out_pre = lax.psum(partial_value.astype(jnp.bfloat16), "ch").astype(jnp.float32) + last_bias
    output = jax.nn.silu(out_pre).astype(jnp.bfloat16)
    grad_out = (
        cotangent.reshape(pixels, out_width).astype(jnp.float32) * scale_loss * silu_slope(out_pre)
    ).astype(jnp.bfloat16)
    grad_last = matmul_rows(mid_act, grad_out)
    grad_side = matmul_rows(own_in, grad_out)
    grad_last_bias = jnp.sum(grad_out.astype(jnp.float32), axis=0)
    mid_back = lax.dot_general(
        grad_out, last_weight, (((1,), (1,)), ((), ())), preferred_element_type=jnp.float32
    )
    mid_delta = (mid_back * silu_slope(mid_pre)).astype(jnp.bfloat16)
    grad_mid = matmul_rows(mid_patches, mid_delta).reshape(3, 3, full_mid, half_mid)
    grad_mid_bias = jnp.sum(mid_delta.astype(jnp.float32), axis=0)
    delta_tiles = mid_delta.reshape(tile_count, extent, extent, half_mid)
    delta_strips = edge_table(delta_tiles).reshape(tile_count, 4, extent * half_mid)
    delta_all = lax.all_gather(delta_strips, "tile", axis=0, tiled=True)
    delta_all = delta_all.reshape(all_tiles, 4, extent, half_mid)
    delta_padded = assemble(delta_tiles, delta_all, neighbours)
    back_patches = patch_cols(delta_padded, BACKWARD_OFFSETS).reshape(pixels, 9 * half_mid)
    w_back = mid_weight.transpose(0, 1, 3, 2).reshape(9 * half_mid, full_mid)
    first_partial = jnp.dot(back_patches, w_back, preferred_element_type=jnp.float32)
    first_partial = first_partial.reshape(tile_count, extent, extent, full_mid)
    first_grad = lax.psum_scatter(first_partial, "ch", scatter_dimension=3, tiled=True)
    own_pre = lax.dynamic_slice_in_dim(first_pre, group_index * half_mid, half_mid, 1)
    first_delta = (first_grad.reshape(pixels, half_mid) * silu_slope(own_pre)).astype(jnp.bfloat16)
    grad_first = matmul_rows(flat_in, first_delta)
    grad_first_bias = jnp.sum(first_delta.astype(jnp.float32), axis=0)
    grad_first, grad_first_bias, grad_mid, grad_mid_bias, grad_last, grad_side, grad_last_bias = (
        lax.psum(
            (
                grad_first,
                grad_first_bias,
                grad_mid,
                grad_mid_bias,
                grad_last,
                grad_side,
                grad_last_bias,
            ),
            "tile",
        )
    )
    output = output.reshape(tile_count, extent, extent, out_width)
    return (
        output,
        grad_first,
        grad_first_bias,
        grad_mid,
        grad_mid_bias,
        grad_last,
        grad_side,
        grad_last_bias,
    )


def solution(mesh):
    return jax.shard_map(
        per_device,
        mesh=mesh,
        in_specs=(
            P("tile", None, None, None),
            P("tile", None, None, None),
            P("tile", None),
            P(),
            P(),
            P(None, None, None, "ch"),
            P(),
            P("ch", None),
            P("ch", None),
            P(),
        ),
        out_specs=(
            P("tile", None, None, None),
            P(None, "ch"),
            P("ch"),
            P(None, None, None, "ch"),
            P("ch"),
            P("ch", None),
            P("ch", None),
            P(),
        ),
        check_vma=False,
    )
```

profile of v0, /device:TPU:1, one launch (start us, length us, event | category | flops | bytes accessed | tf_op | source)
XLA Modules:
  0.0 1161.5 jit_solution(17736341807986507002)
XLA Ops:
  7.2 1.5 copy-done
  8.8 3.4 multiply_convert_fusion.1
  12.2 1.6 copy.79
  19.3 84.6 %all-gather.3.cloned.1.call-done = bf16[256,4,4096]{2,1,0:T(4,128)(2,1)} async-done(((bf16[4,4,4096]{2,1,0:T(4,128)(2,1)}), bf16[256,4,4096]{2,1,0:T(4,128)(2,1)}) %all-gather.3.cloned.1.call-update) | async-done | bytes 8388624 | tf_op jit(solution)/shard_map/all_gather | solution.py:93
  104.0 15.8 %reshape.194 = bf16[256,4,32,128]{3,2,1,0:T(8,128)(2,1)} reshape(bf16[256,4,4096]{2,1,0:T(4,128)(2,1)} %all-gather.3.cloned.1.call-done) | data formatting | bytes 16777216 | tf_op jit(solution)/shard_map/reshape | solution.py:94
  119.8 3.9 gather_fusion.7
  123.7 3.9 gather_fusion.6
  127.6 3.9 gather_fusion.5
  131.6 3.9 gather_fusion.4
  135.5 4.0 gather_fusion.3
  139.5 3.9 gather_fusion.2
  143.4 3.9 gather_fusion.1
  147.4 3.9 gather_fusion
  151.6 2.6 pad_maximum_fusion.4
  154.2 2.3 copy.90
  156.5 2.3 copy.89
  162.6 3.0 pad_maximum_fusion
  165.6 2.3 fusion.43
  167.9 2.3 copy.93
  170.2 2.3 copy.92
  172.5 2.3 copy.91
  174.7 2.4 fusion.44
  177.1 2.3 copy.88
  179.4 2.3 copy.87
  181.7 2.4 copy.86
  189.0 1.8 convolution_add_fusion.1
  190.8 1.8 copy-done.1
  193.9 3.3 add_convert_fusion
  197.5 6.9 convert_multiply_fusion
  204.5 103.8 %all-reduce.13.cloned.1.call-done = bf16[4096,512]{1,0:T(8,128)(2,1)} async-done(((bf16[4096,512]{1,0:T(8,128)(2,1)}), bf16[4096,512]{1,0:T(8,128)(2,1)}) %all-reduce.13.cloned.1.call-update) | async-done | bytes 4194320 | tf_op jit(solution)/shard_map/psum | solution.py:110
  308.3 8.3 convert_reduce_fusion
  316.6 2.3 convert_reduce_fusion.1
  318.9 1.5 copy.95
  322.1 74.8 %all-gather.5.cloned.1.call-done = bf16[256,4,2048]{2,1,0:T(4,128)(2,1)} async-done(((bf16[4,4,2048]{2,1,0:T(4,128)(2,1)}), bf16[256,4,2048]{2,1,0:T(4,128)(2,1)}) %all-gather.5.cloned.1.call-update) | async-done | bytes 4194320 | tf_op jit(solution)/shard_map/all_gather | solution.py:126
  396.9 7.5 copy.97
  404.4 13.0 %copy.98 = bf16[256,4,32,64]{3,2,1,0:T(8,128)(2,1)} copy(bf16[256,4,32,64]{0,3,2,1:T(8,128)(2,1)} %bitcast.94) | data formatting | bytes 8388608 | tf_op jit(solution)/shard_map/reshape | solution.py:127
  417.5 3.9 gather_fusion.15
  421.4 3.9 gather_fusion.14
  425.4 3.9 gather_fusion.13
  429.3 3.9 gather_fusion.12
  433.3 3.9 gather_fusion.11
  437.2 3.9 gather_fusion.10
  441.2 3.9 gather_fusion.9
  445.1 4.0 gather_fusion.8
  449.6 2.3 pad_maximum_fusion.2
  451.9 1.5 maximum_maximum_fusion.1
  453.5 2.4 fusion.41
  455.9 2.3 fusion.42
  458.1 11.9 %concatenate.142 = bf16[4,32,32,576]{3,2,1,0:T(8,128)(2,1)} concatenate(bf16[4,32,32,64]{3,2,1,0:T(8,128)(2,1)} %get-tuple-element.45, bf16[4,32,32,64]{3,2,1,0:T(8,128)(2,1)} %get-tuple-element.44, bf16[4,32,32,64]{3,2,1,0:T(8,128)(2,1)} %get-tuple-element.43, bf16[4,32,32,64]{3,2,1,0:T(8,128)(2,1)} %get-tuple-element.57, bf16[4,32,32,64]{3,2,1,0:T(8,128)(2,1)S(1)} %bitcast.93, ...), dimensions={3} | concatenate | bytes 9437184 | tf_op jit(solution)/shard_map/concatenate | solution.py:48
  470.1 5.4 fusion.47
  475.4 8.4 copy.114
  483.8 7.2 reshape.299
  491.4 3.8 fusion.2
  496.6 7.5 fusion.5
  504.2 17.8 %reduce-scatter.4.cloned.1.call-done = f32[64,4096]{1,0:T(8,128)} async-done(((f32[128,4096]{1,0:T(8,128)}), f32[64,4096]{1,0:T(8,128)}) %reduce-scatter.4.cloned.1.call-update) | async-done | bytes 1048592
  522.0 3.7 reshape.300
  525.7 4.7 copy.115
  530.4 2.2 copy.109
  532.5 1.7 convert_reduce_fusion.2
  535.4 163.2 %all-reduce.8 = (f32[64]{0:T(128)}, f32[64]{0:T(128)}, f32[512]{0:T(512)}) all-reduce(f32[64]{0:T(128)S(1)} %get-tuple-element.37, f32[64]{0:T(128)S(1)} %get-tuple-element.66, f32[512]{0:T(512)S(1)} %get-tuple-element.35), channel_id=1, replica_groups=mesh['tile'=64,'ch'=2] {'tile'}, use_global_device_ids=true, to_apply=%region_4.5 | all-reduce | flops 640 | bytes 5120 | tf_op jit(solution)/shard_map/psum | solution.py:139
  698.6 450.0 %all-reduce.15.cloned.1.call-done = (f32[256,64]{0,1:T(8,128)}, f32[3,3,128,64]{2,3,1,0:T(8,128)}, f32[64,512]{1,0:T(8,128)}, f32[128,512]{1,0:T(8,128)}) async-done(((f32[256,64]{0,1:T(8,128)}, f32[3,3,128,64]{2,3,1,0:T(8,128)}, f32[64,512]{1,0:T(8,128)}, f32[128,512]{1,0:T(8,128)}), (f32[256,64]{0,1:T(8,128)}, f32[3,3,128,64]{2,3,1,0:T(8,128)}, f32[64,512]{1,0:T(8,128)}, ...) | async-done | bytes 753680 | tf_op jit(solution)/shard_map/psum | solution.py:139
  1150.1 1.7 copy.134
  1151.8 1.6 copy.135
  1153.3 1.7 copy.136
  (122 shorter events, 22.3 us)
Async XLA Ops:
  7.2 1.6 copy-start
  7.2 96.8 %all-gather.3.cloned.1.call-start = ((), (), s32[]{:S(2)}) async-start(), calls=%async_computation.1 | async-start | bytes 8519680 | tf_op jit(solution)/shard_map/all_gather | solution.py:93
  8.8 7.8 copy-start.17
  8.8 8.7 copy-start.31
  8.8 9.4 copy-start.19
  13.8 137.8 %copy-start.4 = (bf16[4096,128]{1,0:T(8,128)(2,1)}, bf16[4096,128]{1,0:T(8,128)(2,1)S(1)}, u32[]{:S(2)}) copy-start(bf16[4096,128]{1,0:T(8,128)(2,1)S(1)} %copy.79) | copy-start | bytes 3145732
  16.5 291.8 %all-reduce.13.cloned.1.call-start = ((), (), s32[]{:S(2)}) async-start(), calls=%async_computation.2 | async-start | bytes 8388608 | tf_op jit(solution)/shard_map/psum | solution.py:110
  19.0 140.5 %copy-start.23 = (pred[4]{0:T(512)(128)(4,1)}, pred[4]{0:T(512)(128)(4,1)S(1)}, u32[]{:S(2)}) copy-start(pred[4]{0:T(512)(128)(4,1)S(1)} %get-tuple-element.27) | copy-start | bytes 16
  151.6 10.9 copy-start.16
  181.7 5.4 copy-start.9
  184.1 2.8 copy-start.13
  184.1 3.1 copy-start.7
  185.6 1.7 copy-start.8
  187.0 1.3 copy-start.12
  187.1 1.5 copy-start.11
  187.2 1.7 copy-start.10
  187.3 1.6 copy-start.15
  187.3 1.6 copy-start.30
  189.0 3.6 copy-start.1
  189.0 3.6 copy-start.21
  192.6 124.0 %copy-start.5 = (f32[4096,64]{0,1:T(8,128)}, f32[4096,64]{0,1:T(8,128)S(1)}, u32[]{:S(2)}) copy-start(f32[4096,64]{0,1:T(8,128)S(1)} %convolution_add_fusion.1) | copy-start | bytes 3145732
  192.6 1.3 copy-start.20
  197.2 111.0 %copy-start.29 = (f32[512]{0:T(512)S(1)}, f32[512]{0:T(512)}, u32[]{:S(2)}) copy-start(f32[512]{0:T(512)} %param.19) | copy-start | bytes 6148
  197.3 199.6 %all-gather.5.cloned.1.call-start = ((), (), s32[]{:S(2)}) async-start(), calls=%async_computation.3 | async-start | bytes 4259840 | tf_op jit(solution)/shard_map/all_gather | solution.py:126
  316.6 2.3 copy-start.2
  322.0 200.0 %reduce-scatter.4.cloned.1.call-start = ((), (), s32[]{:S(2)}) async-start(), calls=%async_computation.4 | async-start | bytes 3145728
  404.4 44.7 %copy-start.27 = (pred[4]{0:T(512)(128)(4,1)S(1)}, pred[4]{0:T(512)(128)(4,1)}, u32[]{:S(2)}) copy-start(pred[4]{0:T(512)(128)(4,1)} %get-tuple-element.23) | copy-start | bytes 16
  404.4 44.7 %copy-start.28 = (pred[4]{0:T(512)(128)(4,1)S(1)}, pred[4]{0:T(512)(128)(4,1)}, u32[]{:S(2)}) copy-start(pred[4]{0:T(512)(128)(4,1)} %get-tuple-element.25) | copy-start | bytes 16
  404.4 44.8 %copy-start.22 = (pred[4]{0:T(512)(128)(4,1)S(1)}, pred[4]{0:T(512)(128)(4,1)}, u32[]{:S(2)}) copy-start(pred[4]{0:T(512)(128)(4,1)} %get-tuple-element.24) | copy-start | bytes 16
  404.4 44.8 %copy-start.24 = (pred[4]{0:T(512)(128)(4,1)S(1)}, pred[4]{0:T(512)(128)(4,1)}, u32[]{:S(2)}) copy-start(pred[4]{0:T(512)(128)(4,1)} %copy-done.23) | copy-start | bytes 16
  404.4 44.9 %copy-start.25 = (pred[4]{0:T(512)(128)(4,1)S(1)}, pred[4]{0:T(512)(128)(4,1)}, u32[]{:S(2)}) copy-start(pred[4]{0:T(512)(128)(4,1)} %get-tuple-element.20) | copy-start | bytes 16
  404.4 44.9 %copy-start.26 = (pred[4]{0:T(512)(128)(4,1)S(1)}, pred[4]{0:T(512)(128)(4,1)}, u32[]{:S(2)}) copy-start(pred[4]{0:T(512)(128)(4,1)} %get-tuple-element.26) | copy-start | bytes 16
  458.1 11.9 %copy-start.18 = (bf16[3,3,128,64]{2,3,1,0:T(8,128)(2,1)S(1)}, bf16[3,3,128,64]{2,3,1,0:T(8,128)(2,1)}, u32[]{:S(2)}) copy-start(bf16[3,3,128,64]{2,3,1,0:T(8,128)(2,1)} %param.15) | copy-start | bytes 442372
  491.1 4.1 copy-start.6
  491.1 657.5 %all-reduce.15.cloned.1.call-start = ((), (), s32[]{:S(2)}) async-start(), calls=%async_computation.5 | async-start | bytes 1507328 | tf_op jit(solution)/shard_map/psum | solution.py:139
  491.4 3.8 copy-start.3
  495.2 1.4 copy-start.14
Sparse Core Ops, SparseCore 0:
  16.6 87.2 all-gather.2
  197.4 110.8 all-reduce.12
  322.1 74.7 all-gather.4
  491.2 30.7 reduce-scatter.3
  535.5 612.9 all-reduce.14
where the time goes:
time: 1170 us; the launch traced here: 1160 us
  waiting for transfers between devices  731 us (62%)
  local copies, waits for them, and re-layouts  188 us (16%)
  blocking collectives  163 us (14%)
  other arithmetic  33 us (3%)
  matrix products  31.3 us (3%)
  between operations  14.3 us (1%)
    psum x1, waiting for transfers between devices, per_device(): lax.psum((grad_first, grad_first_bias, grad_mid, grad_mid_bias, grad_last...  450 us
    psum x1, blocking collectives, per_device(): lax.psum((grad_first, grad_first_bias, grad_mid, grad_mid_bias, grad_last...  163 us
    psum x1, waiting for transfers between devices, per_device(): lax.psum(partial_value.astype(jnp.bfloat16), 'ch').astype(jnp.float32)  104 us
    all_gather x1, waiting for transfers between devices, per_device(): strip_all = lax.all_gather(strips_out, 'tile', axis=0, tiled=True)  84.6 us
    all_gather x1, waiting for transfers between devices, per_device(): delta_all = lax.all_gather(delta_strips, 'tile', axis=0, tiled=True)  74.8 us
    gather x16, local copies, waits for them, and re-layouts, choose_strip(): strips = strip_table[jnp.minimum(owner_ids, table_size - 1), strip_id]  63.2 us
    unnamed x81, local copies, waits for them, and re-layouts  38.6 us
    concatenate x10, local copies, waits for them, and re-layouts, patch_cols(): jnp.concatenate([padded_in[:, row_off:row_off + extent, col_off:col_off +...  30.4 us
  transfers between devices with their start and end apart: 5, of which 5 were waited for; matrix products, arithmetic and copies ran while one was open for 2% of the time, Pallas kernels for 0%

commit v1 on v0

v1 whole, which is shorter than its diff:
```python
import math

import jax
import jax.numpy as jnp
from jax import lax
from jax.experimental import pallas as pl
from jax.experimental.pallas import tpu as pltpu
from jax.sharding import PartitionSpec as P

BF = jnp.bfloat16
F32 = jnp.float32
MESH = pl.DeviceIdType.MESH

ROW_FIRST = 0
ROW_MID = 128
ROW_LAST = 704
ROW_SIDE = 960
ROW_BIAS = 1472
ROWS = 1536
CORE_ROWS = ROWS // 2
PIECE = CORE_ROWS // 16

CHUNK = 256


def place():
    tile = lax.axis_index("tile")
    ch = lax.axis_index("ch")
    return tile // 16, (tile // 8) % 2, (tile // 2) % 4, tile % 2, ch


def device(y, zh, x, core, ch):
    return (((y * 2 + zh) * 4 + x) * 2 + core, ch)


def exchange_kernel(
    feat,
    near,
    wb_own,
    wl_own,
    ws_own,
    halo,
    wb_other,
    wl_other,
    ws_other,
    wide,
    edges,
    table,
    table_s,
    every,
    pack,
    got,
    piece,
    send_sem,
    recv_sem,
    local_sem,
):
    y, zh, x, core, ch = place()
    along = jnp.where(core == 0, x, y)
    across = jnp.where(core == 0, y, x)

    def gather_peer(step):
        to = lax.rem(along + step, 4)
        return device(jnp.where(core == 0, y, to), zh, jnp.where(core == 0, to, x), core, ch)

    def select_peer(step):
        to = lax.rem(across + step, 4)
        return device(jnp.where(core == 0, to, y), zh, jnp.where(core == 0, x, to), core, ch)

    sibling = device(y, zh, x, 1 - core, ch)
    z_peers = [device(y, 1 - zh, x, role, 1 - ch) for role in (0, 1)]
    z_same = device(y, 1 - zh, x, core, 1 - ch)
    z_cross = device(y, 1 - zh, x, 1 - core, 1 - ch)
    ch_same = device(y, zh, x, core, 1 - ch)
    ch_cross = device(y, zh, x, 1 - core, 1 - ch)

    barrier = pltpu.get_barrier_semaphore()
    greeted = [sibling, z_same, z_cross, ch_same, ch_cross]
    greeted += [gather_peer(1), gather_peer(3)]
    greeted += [select_peer(1), select_peer(2), select_peer(3)]
    for peer in greeted:
        pl.semaphore_signal(barrier, inc=1, device_id=peer, device_id_type=MESH)

    table[across, core] = jnp.zeros((8, 128), jnp.int32)
    table[across, core, 0:4, 0:8] = near[...]

    for tile in range(4):
        first_row = feat[tile, 0]
        last_row = feat[tile, 31]
        for half in range(2):
            lanes = slice(half * 128, half * 128 + 128)
            wide[0:512, :] = feat[tile, :, 0:16, lanes].astype(F32).reshape(512, 128)
            wide[512:1024, :] = feat[tile, :, 16:32, lanes].astype(F32).reshape(512, 128)
            edges[0, half, tile, 0] = first_row[:, lanes]
            edges[0, half, tile, 1] = last_row[:, lanes]
            edges[1, half, tile, 0] = wide[pl.ds(0, 32, stride=16), :].astype(BF)
            edges[1, half, tile, 1] = wide[pl.ds(527, 32, stride=16), :].astype(BF)
    every[zh, along, core] = edges[core, ch]

    pl.semaphore_wait(barrier, len(greeted))

    def copy(number, source, target, peer, arrives):
        return pltpu.make_async_remote_copy(
            src_ref=source,
            dst_ref=target,
            send_sem=send_sem.at[number],
            recv_sem=recv_sem.at[arrives],
            device_id=peer,
            device_id_type=MESH,
        )

    sent = []

    def start(number, source, target, peer, arrives):
        made = copy(number, source, target, peer, arrives)
        made.start()
        sent.append(made)
        return made

    tab = start(0, table.at[across, core], table.at[across_of(1 - core, x, y), core], sibling, 0)
    sib_along = jnp.where(core == 0, y, x)
    start(1, edges.at[1 - core, ch], every.at[zh, sib_along, core], sibling, 1)
    for role in range(2):
        place_along = x if role == 0 else y
        start(
            2 + role,
            edges.at[role, 1 - ch],
            every.at[zh, place_along, core],
            z_peers[role],
            2 + core,
        )
    start(4, wb_own, wb_other, ch_same, 4)
    start(5, wl_own, wl_other, ch_same, 5)
    start(6, ws_own, ws_other, ch_same, 6)

    def arrived(number, target):
        copy(0, target, target, sibling, number).wait_recv()

    arrived(1, every.at[zh, along, 1 - core])
    start(7, every.at[zh, along], every.at[zh, along], gather_peer(1), 7)
    start(8, every.at[zh, along], every.at[zh, along], gather_peer(3), 8)
    arrived(0, table.at[across, 1 - core])
    for step in range(1, 4):
        start(8 + step, table.at[across], table.at[across], select_peer(step), 8 + step)
    arrived(2, every.at[1 - zh, along, 0])
    arrived(3, every.at[1 - zh, along, 1])
    start(12, every.at[1 - zh, along], every.at[1 - zh, along], gather_peer(1), 12)
    start(13, every.at[1 - zh, along], every.at[1 - zh, along], gather_peer(3), 13)
    before = lax.rem(along + 3, 4)
    after = lax.rem(along + 1, 4)
    opposite = lax.rem(along + 2, 4)
    for plane, first, second in ((zh, 7, 14), (1 - zh, 12, 16)):
        arrived(first, every.at[plane, before])
        start(
            second, every.at[plane, before, 0], every.at[plane, before, 0], gather_peer(1), second
        )
        arrived(first + 1, every.at[plane, after])
        start(
            second + 1,
            every.at[plane, after, 1],
            every.at[plane, after, 1],
            gather_peer(3),
            second + 1,
        )
    for step in range(1, 4):
        arrived(8 + step, table.at[lax.rem(across + 4 - step, 4)])
    local = pltpu.make_async_copy(table, table_s, local_sem)
    local.start()
    local.wait()
    for second, plane in ((14, zh), (16, 1 - zh)):
        arrived(second, every.at[plane, opposite, 0])
        arrived(second + 1, every.at[plane, opposite, 1])

    first_dir = 1 + 2 * core
    second_dir = 6 - 2 * core
    rows16 = lax.broadcasted_iota(jnp.int32, (16, 128), 0)

    def strip(tile_id, which, rows=slice(0, 32)):
        n = jnp.minimum(tile_id, 255)
        held_along = jnp.where(core == 0, (n // 8) % 4, n // 64)
        return every[(n // 32) % 2, held_along, (n // 4) % 2, n % 4, which, rows, :]

    def source(tile_id):
        n = jnp.minimum(tile_id, 255)
        return jnp.where(core == 0, n // 64, (n // 8) % 4)

    for step in (1, 3, 2, 0):
        wanted = lax.rem(across + step, 4)

        def pack_tile(number, carry, wanted=wanted, step=step):
            owner, tile = number // 4, number % 4
            ids = lambda d: table_s[wanted, owner, tile, d]
            one = strip(ids(first_dir), 1)
            two = strip(ids(second_dir), 0)
            up_left = strip(ids(0), 1, slice(16, 32)).astype(F32)[15:16]
            up_right = strip(ids(2), 1, slice(0, 16)).astype(F32)[0:1]
            down_left = strip(ids(5), 0, slice(16, 32)).astype(F32)[15:16]
            down_right = strip(ids(7), 0, slice(0, 16)).astype(F32)[0:1]
            corners = jnp.where(
                rows16 == 0,
                up_left,
                jnp.where(
                    rows16 == 1,
                    up_right,
                    jnp.where(rows16 == 2, down_left, jnp.where(rows16 == 3, down_right, 0.0)),
                ),
            )
            pack[step, owner, tile, 0:32, :] = one
            pack[step, owner, tile, 32:64, :] = two
            pack[step, owner, tile, 64:80, :] = corners.astype(BF)
            return carry

        lax.fori_loop(0, 8, pack_tile, 0)
        if step:
            start(17 + step, pack.at[step], got.at[step], select_peer(step), 17 + step)
    for step in range(1, 4):
        arrived(17 + step, got.at[step])

    def take(tile_id):
        return lax.rem(across + 4 - source(tile_id), 4)

    def finish_tile(number, carry):
        owner, tile = number // 4, number % 4
        ids = lambda d: table_s[across, owner, tile, d]

        def chosen(d, rows):
            return got[take(ids(d)), owner, tile, rows, :]

        one = chosen(first_dir, slice(0, 32))
        two = chosen(second_dir, slice(32, 64))
        end = slice(64, 80)
        corners = jnp.where(
            rows16 == 0,
            chosen(0, end).astype(F32),
            jnp.where(
                rows16 == 1,
                chosen(2, end).astype(F32),
                jnp.where(rows16 == 2, chosen(5, end).astype(F32), chosen(7, end).astype(F32)),
            ),
        )
        piece[owner, tile, 0:32, :] = one
        piece[owner, tile, 32:64, :] = two
        piece[owner, tile, 64:80, :] = corners.astype(BF)
        return carry

    got[0] = pack[0]
    lax.fori_loop(0, 8, finish_tile, 0)
    halo[core, ch] = piece[core]
    start(21, piece.at[1 - core], halo.at[core, ch], sibling, 21)
    start(22, piece.at[core], halo.at[core, ch], ch_same, 22)
    start(23, piece.at[1 - core], halo.at[core, ch], ch_cross, 23)
    arrived(21, halo.at[1 - core, ch])
    arrived(22, halo.at[core, 1 - ch])
    arrived(23, halo.at[1 - core, 1 - ch])
    arrived(4, wb_other)
    arrived(5, wl_other)
    arrived(6, ws_other)
    for made in sent:
        made.wait_send()


def across_of(core, x, y):
    return jnp.where(core == 0, y, x)


def exchange(features, neighbours, wb_own, wl_own, ws_own):
    vmem = pl.BlockSpec(memory_space=pltpu.VMEM)
    return pl.pallas_call(
        exchange_kernel,
        out_shape=(
            jax.ShapeDtypeStruct((2, 2, 4, 80, 128), BF),
            jax.ShapeDtypeStruct(wb_own.shape, BF),
            jax.ShapeDtypeStruct(wl_own.shape, BF),
            jax.ShapeDtypeStruct(ws_own.shape, BF),
        ),
        in_specs=[vmem] * 5,
        out_specs=(vmem,) * 4,
        scratch_shapes=[
            pltpu.VMEM((1024, 128), F32),
            pltpu.VMEM((2, 2, 4, 2, 32, 128), BF),
            pltpu.VMEM((4, 2, 8, 128), jnp.int32),
            pltpu.SMEM((4, 2, 8, 128), jnp.int32),
            pltpu.VMEM((2, 4, 2, 4, 2, 32, 128), BF),
            pltpu.VMEM((4, 2, 4, 80, 128), BF),
            pltpu.VMEM((4, 2, 4, 80, 128), BF),
            pltpu.VMEM((2, 4, 80, 128), BF),
            pltpu.SemaphoreType.DMA((24,)),
            pltpu.SemaphoreType.DMA((24,)),
            pltpu.SemaphoreType.DMA,
        ],
        compiler_params=pltpu.CompilerParams(
            collective_id=0, has_side_effects=True, vmem_limit_bytes=48 * 2**20
        ),
    )(features, neighbours, wb_own, wl_own, ws_own)


def sigmoid(v):
    return 0.5 + 0.5 * jnp.tanh(0.5 * v)


def dot(a, b):
    return jnp.dot(a, b, preferred_element_type=F32)


def dot_nt(a, b):
    return lax.dot_general(a, b, (((1,), (1,)), ((), ())), preferred_element_type=F32)


def dot_tn(a, b):
    return lax.dot_general(a, b, (((0,), (0,)), ((), ())), preferred_element_type=F32)


def compute_kernel(
    scale,
    ch_s,
    near_s,
    feat,
    cot,
    halo,
    w1,
    b1,
    wb_own,
    wb_other,
    mid_bias,
    wl_own,
    wl_other,
    ws_own,
    ws_other,
    last_bias,
    out,
    grads,
    wf,
    wbt,
    wl,
    ws,
    first_pre,
    side_pre,
    padded,
    patches,
    mid_delta,
    spread,
    rim,
    g_first,
    g_mid,
    g_last,
    g_side,
    g_first_bias,
    g_mid_bias,
    g_last_bias,
):
    step = pl.program_id(0)
    ch = ch_s[0]
    tile = lax.rem(step + 2 * ch, 4)
    own64 = pl.multiple_of(ch * 64, 64)
    other64 = pl.multiple_of((1 - ch) * 64, 64)
    own128 = pl.multiple_of(ch * 128, 128)
    other128 = pl.multiple_of((1 - ch) * 128, 128)

    @pl.when(step == 0)
    def _():
        for i in range(3):
            lanes = slice(i * 384, i * 384 + 384)
            rows = jnp.concatenate([wb_own[:, lanes], wb_other[:, lanes]], axis=0)
            wbt[i * 128 : i * 128 + 128, :] = rows
            wf[i] = rows.astype(F32).T.astype(BF)
        wl[0:64, :] = wl_own[...]
        wl[64:128, :] = wl_other[...]
        ws[pl.ds(own128, 128), :] = ws_own[...]
        ws[pl.ds(other128, 128), :] = ws_other[...]
        for ref in (g_first, g_mid, g_last, g_side, g_first_bias, g_mid_bias, g_last_bias):
            ref[...] = jnp.zeros_like(ref)

    def here(direction):
        return jnp.where(near_s[tile, direction] < 256, 1.0, 0.0).astype(F32)

    x_own = feat[...]
    pre = dot(x_own, w1[...]) + b1[...]
    first_pre[...] = pre
    act = pre * sigmoid(pre)
    padded[1:33, 8:40, :] = act.reshape(32, 32, 128)
    x_rim = jnp.concatenate(
        [
            jnp.concatenate([halo[0, 0, 0], halo[0, 1, 0]], axis=1),
            jnp.concatenate([halo[1, 0, 0], halo[1, 1, 0]], axis=1),
        ],
        axis=0,
    )
    pre = dot(x_rim, w1[...]) + b1[...]
    side_pre[...] = pre
    act = pre * sigmoid(pre)
    padded[0, 8:40, :] = act[0:32] * here(1)
    padded[33, 8:40, :] = act[32:64] * here(6)
    rim[...] = act
    padded[1:33, 7:8, :] = (act[80:112] * here(3)).reshape(32, 1, 128)
    padded[1:33, 40:41, :] = (act[112:144] * here(4)).reshape(32, 1, 128)
    padded[0, 7:8, :] = rim[64:65, :] * here(0)
    padded[0, 40:41, :] = rim[65:66, :] * here(2)
    padded[33, 7:8, :] = rim[66:67, :] * here(5)
    padded[33, 40:41, :] = rim[67:68, :] * here(7)
    for j in range(3):
        patches[:, :, j * 128 : j * 128 + 128] = padded[:, 7 + j : 39 + j, :].astype(BF)

    def forward(number):
        row = pl.multiple_of(number * CHUNK, CHUNK)
        high = CHUNK // 32
        line = number * high
        views = [patches[pl.ds(line + i, high)].reshape(CHUNK, 384) for i in range(3)]
        mid_pre = mid_bias[...] + dot(views[0], wf[0]) + dot(views[1], wf[1]) + dot(views[2], wf[2])
        mid_sig = sigmoid(mid_pre)
        mid_val = mid_pre * mid_sig
        mid_act = mid_val.astype(BF)
        x_part = feat[pl.ds(row, CHUNK), :]
        out_pre = dot(mid_act, wl[...]) + dot(x_part, ws[...]) + last_bias[...]
        sig = sigmoid(out_pre)
        val = out_pre * sig
        out[pl.ds(row, CHUNK), :] = val.astype(BF)
        return row, views, mid_sig, mid_val, mid_act, x_part, sig, val

    @pl.when(step >= 2)
    def _():
        def body(number, carry):
            forward(number)
            return carry

        lax.fori_loop(0, 1024 // CHUNK, body, 0)

    @pl.when(step < 2)
    def _():
        def body(number, carry):
            row, views, mid_sig, mid_val, mid_act, x_part, sig, val = forward(number)
            slope = sig + val * (1.0 - sig)
            grad_out = (cot[pl.ds(row, CHUNK), :].astype(F32) * scale * slope).astype(BF)
            g_last[...] += dot_tn(mid_act, grad_out)
            g_side[...] += dot_tn(x_part, grad_out)
            g_last_bias[...] += grad_out.astype(F32).reshape(CHUNK // 8, 8, 512).sum(axis=0)
            mid_back = dot_nt(grad_out, wl[...])
            delta = (mid_back * (mid_sig + mid_val * (1.0 - mid_sig))).astype(BF)
            g_mid_bias[...] += delta.astype(F32).reshape(CHUNK // 8, 8, 128).sum(axis=0)
            for i in range(3):
                g_mid[i] += dot_tn(delta, views[i])
            high = CHUNK // 32
            line = number * high
            for i in range(3):
                mid_delta[pl.ds(line + i, high), :, i * 128 : i * 128 + 128] = delta.reshape(
                    high, 32, 128
                )
            return carry

        blank = jnp.zeros((32, 128), BF)
        mid_delta[32, :, 0:128] = blank
        mid_delta[33, :, 0:128] = blank
        mid_delta[0, :, 128:256] = blank
        mid_delta[33, :, 128:256] = blank
        mid_delta[0, :, 256:384] = blank
        mid_delta[1, :, 256:384] = blank
        lax.fori_loop(0, 1024 // CHUNK, body, 0)

        back = dot(mid_delta[...].reshape(1088, 384), wbt[...]).reshape(34, 32, 384)
        spread[:, 0:8, :] = jnp.zeros((34, 8, 128), F32)
        spread[:, 40:48, :] = jnp.zeros((34, 8, 128), F32)
        spread[:, 8:40, :] = back[:, :, 128:256]
        spread[:, 7:39, :] += back[:, :, 0:128]
        spread[:, 9:41, :] += back[:, :, 256:384]

        pre = first_pre[...]
        sig = sigmoid(pre)
        slope = sig + pre * sig * (1.0 - sig)
        delta = (spread[1:33, 8:40, :].reshape(1024, 128) * slope).astype(BF)
        rim[...] = jnp.zeros_like(rim)
        rim[0:32, :] = spread[0, 8:40, :] * here(1)
        rim[32:64, :] = spread[33, 8:40, :] * here(6)
        rim[64:65, :] = spread[0, 7:8, :] * here(0)
        rim[65:66, :] = spread[0, 40:41, :] * here(2)
        rim[66:67, :] = spread[33, 7:8, :] * here(5)
        rim[67:68, :] = spread[33, 40:41, :] * here(7)
        rim[80:112, :] = spread[1:33, 7:8, :].reshape(32, 128) * here(3)
        rim[112:144, :] = spread[1:33, 40:41, :].reshape(32, 128) * here(4)
        pre = side_pre[...]
        sig = sigmoid(pre)
        slope = sig + pre * sig * (1.0 - sig)
        delta_rim = (rim[...] * slope).astype(BF)
        g_first[...] += dot_tn(delta, x_own) + dot_tn(delta_rim, x_rim)
        g_first_bias[...] += delta.astype(F32).reshape(128, 8, 128).sum(axis=0)
        g_first_bias[...] += delta_rim.astype(F32).reshape(20, 8, 128).sum(axis=0)

    @pl.when(step == 1)
    def _():
        bias_first = jnp.sum(g_first_bias[...], axis=0, keepdims=True)
        bias_mid = jnp.sum(g_mid_bias[...], axis=0, keepdims=True)
        bias_last = jnp.sum(g_last_bias[...], axis=0, keepdims=True)
        rows16 = lax.broadcasted_iota(jnp.int32, (16, 128), 0)
        for half in range(2):
            start64 = own64 if half == 0 else other64
            start128 = own128 if half == 0 else other128
            order = slice(half * 64, half * 64 + 64)
            for k in range(2):
                at = ROW_FIRST + k * 64
                grads[half, at : at + 64, :] = g_first[
                    pl.ds(start64, 64), k * 128 : k * 128 + 128
                ].astype(BF)
            for i in range(3):
                for j in range(3):
                    at = ROW_MID + (i * 3 + j) * 64
                    grads[half, at : at + 64, :] = g_mid[i, order, j * 128 : j * 128 + 128].astype(
                        BF
                    )
            for k in range(4):
                lanes = slice(k * 128, k * 128 + 128)
                at = ROW_LAST + k * 64
                grads[half, at : at + 64, :] = g_last[order, lanes].astype(BF)
                at = ROW_SIDE + k * 128
                grads[half, at : at + 128, :] = g_side[pl.ds(start128, 128), lanes].astype(BF)
            mid_row = bias_mid
            if half == 1:
                mid_row = jnp.concatenate([bias_mid[:, 64:128], bias_mid[:, 0:64]], axis=1)
            rows = jnp.where(rows16 == 0, bias_first, jnp.where(rows16 == 1, mid_row, 0.0))
            for k in range(4):
                rows = jnp.where(rows16 == 2 + k, bias_last[:, k * 128 : k * 128 + 128], rows)
            grads[half, ROW_BIAS : ROW_BIAS + 16, :] = rows.astype(BF)
            grads[half, ROW_BIAS + 16 : ROWS, :] = jnp.zeros((ROWS - ROW_BIAS - 16, 128), BF)


def compute(
    scale,
    ch,
    neighbours,
    features,
    cotangent,
    halo,
    w1,
    b1,
    wb_own,
    wb_other,
    mid_bias,
    wl_own,
    wl_other,
    ws_own,
    ws_other,
    last_bias,
):
    def whole(shape):
        zeros = (0,) * len(shape)
        return pl.BlockSpec(shape, lambda s, c, n: zeros)

    def tile_at(s, c):
        return lax.rem(s + 2 * c[0], 4)

    grid_spec = pltpu.PrefetchScalarGridSpec(
        num_scalar_prefetch=2,
        grid=(4,),
        in_specs=[
            pl.BlockSpec((1024, 256), lambda s, c, n: (tile_at(s, c), 0)),
            pl.BlockSpec((1024, 512), lambda s, c, n: (2 * c[0] + jnp.minimum(s, 1), 0)),
            pl.BlockSpec((2, 2, 1, 80, 128), lambda s, c, n: (0, 0, tile_at(s, c), 0, 0)),
            whole((256, 128)),
            whole((1, 128)),
            whole((64, 1152)),
            whole((64, 1152)),
            whole((1, 128)),
            whole((64, 512)),
            whole((64, 512)),
            whole((128, 512)),
            whole((128, 512)),
            whole((1, 512)),
        ],
        out_specs=(
            pl.BlockSpec((1024, 512), lambda s, c, n: (tile_at(s, c), 0)),
            whole((2, ROWS, 128)),
        ),
        scratch_shapes=[
            pltpu.VMEM((3, 384, 128), BF),
            pltpu.VMEM((384, 384), BF),
            pltpu.VMEM((128, 512), BF),
            pltpu.VMEM((256, 512), BF),
            pltpu.VMEM((1024, 128), F32),
            pltpu.VMEM((160, 128), F32),
            pltpu.VMEM((34, 48, 128), F32),
            pltpu.VMEM((34, 32, 384), BF),
            pltpu.VMEM((34, 32, 384), BF),
            pltpu.VMEM((34, 48, 128), F32),
            pltpu.VMEM((160, 128), F32),
            pltpu.VMEM((128, 256), F32),
            pltpu.VMEM((3, 128, 384), F32),
            pltpu.VMEM((128, 512), F32),
            pltpu.VMEM((256, 512), F32),
            pltpu.VMEM((8, 128), F32),
            pltpu.VMEM((8, 128), F32),
            pltpu.VMEM((8, 512), F32),
        ],
    )

    def kernel(*refs):
        compute_kernel(scale, *refs)

    return pl.pallas_call(
        kernel,
        grid_spec=grid_spec,
        out_shape=(
            jax.ShapeDtypeStruct((4096, 512), BF),
            jax.ShapeDtypeStruct((2, ROWS, 128), BF),
        ),
        compiler_params=pltpu.CompilerParams(vmem_limit_bytes=56 * 2**20),
    )(
        ch,
        neighbours,
        features,
        cotangent,
        halo,
        w1,
        b1,
        wb_own,
        wb_other,
        mid_bias,
        wl_own,
        wl_other,
        ws_own,
        ws_other,
        last_bias,
    )


def reduce_kernel(grads, total, from_core, by_piece, from_plane, mine, from_z, done, send_sem, recv_sem):
    y, zh, x, core, ch = place()
    own = y * 4 + x
    sibling = device(y, zh, x, 1 - core, ch)

    def plane_peer(step):
        to = lax.rem(own + step, 16)
        return device(to // 4, zh, to % 4, core, ch)

    z_same = device(y, 1 - zh, x, core, ch)
    ch_same = device(y, zh, x, core, 1 - ch)
    z_cross = device(y, 1 - zh, x, core, 1 - ch)
    last = [z_same, ch_same, z_cross]

    barrier = pltpu.get_barrier_semaphore()
    greeted = [sibling, *last] + [plane_peer(step) for step in range(1, 16)]
    for peer in greeted:
        pl.semaphore_signal(barrier, inc=1, device_id=peer, device_id_type=MESH)
    pl.semaphore_wait(barrier, len(greeted))

    def copy(number, source, target, peer):
        return pltpu.make_async_remote_copy(
            src_ref=source,
            dst_ref=target,
            send_sem=send_sem.at[number],
            recv_sem=recv_sem.at[number],
            device_id=peer,
            device_id_type=MESH,
        )

    own_rows = pl.multiple_of(core * CORE_ROWS, CORE_ROWS)
    other_rows = pl.multiple_of((1 - core) * CORE_ROWS, CORE_ROWS)
    swap = copy(0, grads.at[:, pl.ds(other_rows, CORE_ROWS)], from_core, sibling)
    swap.start()
    swap.wait()
    for half in range(2):
        added = grads[half, pl.ds(own_rows, CORE_ROWS), :].astype(F32) + from_core[half].astype(F32)
        by_piece[:, half] = added.astype(BF).reshape(16, PIECE, 128)
    copies = []
    for step in range(1, 16):
        to = lax.rem(own + step, 16)
        made = copy(step, by_piece.at[to], from_plane.at[step], plane_peer(step))
        made.start()
        copies.append(made)
    added = by_piece[own].astype(F32)
    for step, made in enumerate(copies, 1):
        made.wait_recv()
        added = added + from_plane[step].astype(F32)
    mine[...] = added.astype(BF)
    halves = (0, 1, 1)
    hops = []
    for k in range(3):
        made = copy(16 + k, mine.at[halves[k]], from_z.at[k], last[k])
        made.start()
        hops.append(made)
    added = added[0]
    for k, made in enumerate(hops):
        made.wait_recv()
        added = added + from_z[k].astype(F32)
    at = own_rows + own * PIECE
    at = pl.multiple_of(at, 16)
    done[pl.ds(at, PIECE), :] = added.astype(BF)
    backs = []
    for step in range(1, 16):
        made = copy(18 + step, done.at[pl.ds(at, PIECE)], done.at[pl.ds(at, PIECE)], plane_peer(step))
        made.start()
        backs.append(made)
    for made in backs:
        made.wait_recv()
    final = copy(34, done.at[pl.ds(own_rows, CORE_ROWS)], done.at[pl.ds(own_rows, CORE_ROWS)], sibling)
    final.start()
    final.wait_recv()
    total[...] = done[...]
    for made in [*copies, *hops, *backs, final]:
        made.wait_send()


def reduce_gradients(grads):
    vmem = pl.BlockSpec(memory_space=pltpu.VMEM)
    return pl.pallas_call(
        reduce_kernel,
        out_shape=jax.ShapeDtypeStruct((ROWS, 128), BF),
        in_specs=[vmem],
        out_specs=vmem,
        scratch_shapes=[
            pltpu.VMEM((2, CORE_ROWS, 128), BF),
            pltpu.VMEM((16, 2, PIECE, 128), BF),
            pltpu.VMEM((16, 2, PIECE, 128), BF),
            pltpu.VMEM((2, PIECE, 128), BF),
            pltpu.VMEM((3, PIECE, 128), BF),
            pltpu.VMEM((ROWS, 128), BF),
            pltpu.SemaphoreType.DMA((35,)),
            pltpu.SemaphoreType.DMA((35,)),
        ],
        compiler_params=pltpu.CompilerParams(
            collective_id=1, has_side_effects=True, vmem_limit_bytes=32 * 2**20
        ),
    )(grads)


def unpack_kernel(ch_s, total, g_first, g_first_bias, g_mid, g_mid_bias, g_last, g_side, g_last_bias):
    def rows(at, count):
        return total[at : at + count, :].astype(F32)

    for k in range(2):
        g_first[k * 128 : k * 128 + 128, :] = rows(ROW_FIRST + k * 64, 64).T
    for k in range(9):
        g_mid[k // 3, k % 3] = rows(ROW_MID + k * 64, 64).T
    bias = rows(ROW_BIAS, 16)
    for k in range(4):
        lanes = slice(k * 128, k * 128 + 128)
        g_last[:, lanes] = rows(ROW_LAST + k * 64, 64)
        g_side[:, lanes] = rows(ROW_SIDE + k * 128, 128)
        g_last_bias[:, lanes] = bias[2 + k : 3 + k, :]
    g_first_bias[...] = jnp.where(ch_s[0] == 0, bias[0:1, 0:64], bias[0:1, 64:128])
    g_mid_bias[...] = bias[1:2, 0:64]


def unpack(ch, total):
    vmem = pl.BlockSpec(memory_space=pltpu.VMEM)
    return pl.pallas_call(
        unpack_kernel,
        in_specs=[pl.BlockSpec(memory_space=pltpu.SMEM), vmem],
        out_specs=(vmem,) * 7,
        out_shape=tuple(
            jax.ShapeDtypeStruct(shape, F32)
            for shape in (
                (256, 64),
                (1, 64),
                (3, 3, 128, 64),
                (1, 64),
                (64, 512),
                (128, 512),
                (1, 512),
            )
        ),
        compiler_params=pltpu.CompilerParams(vmem_limit_bytes=32 * 2**20),
    )(ch, total)


def per_device(
    features,
    cotangent,
    neighbours,
    first_weight,
    first_bias,
    mid_weight,
    mid_bias,
    last_weight,
    side_weight,
    last_bias,
):
    scale = 1.0 / math.sqrt(4096)
    which = lax.axis_index("ch")
    ch = which.astype(jnp.int32).reshape(1)
    wb_own = mid_weight.transpose(3, 0, 1, 2).reshape(64, 1152)
    swapped = jnp.concatenate([mid_bias[64:], mid_bias[:64]])
    own_first = jnp.where(which == 0, mid_bias, swapped).reshape(1, 128)
    halo, wb_other, wl_other, ws_other = exchange(
        features, neighbours, wb_own, last_weight, side_weight
    )
    output, grads = compute(
        scale,
        ch,
        neighbours,
        features.reshape(4096, 256),
        cotangent.reshape(4096, 512),
        halo,
        first_weight,
        first_bias.reshape(1, 128),
        wb_own,
        wb_other,
        own_first,
        last_weight,
        wl_other,
        side_weight,
        ws_other,
        last_bias.reshape(1, 512),
    )
    total = reduce_gradients(grads)
    g_first, g_first_bias, g_mid, g_mid_bias, g_last, g_side, g_last_bias = unpack(ch, total)
    return (
        output.reshape(4, 32, 32, 512),
        g_first,
        g_first_bias.reshape(64),
        g_mid,
        g_mid_bias.reshape(64),
        g_last,
        g_side,
        g_last_bias.reshape(512),
    )


def solution(mesh):
    return jax.shard_map(
        per_device,
        mesh=mesh,
        in_specs=(
            P("tile", None, None, None),
            P("tile", None, None, None),
            P("tile", None),
            P(),
            P(),
            P(None, None, None, "ch"),
            P(),
            P("ch", None),
            P("ch", None),
            P(),
        ),
        out_specs=(
            P("tile", None, None, None),
            P(None, "ch"),
            P("ch"),
            P(None, None, None, "ch"),
            P("ch"),
            P("ch", None),
            P("ch", None),
            P(),
        ),
        check_vma=False,
    )
```

time: 1170 us -> 95.7 us (0.08)
  waiting for transfers between devices: 731 us -> 0 us
  local copies, waits for them, and re-layouts: 188 us -> 11.4 us
  blocking collectives: 163 us -> 0 us
  Pallas kernels: 0 us -> 81.9 us
  other arithmetic: 33 us -> 1.24 us
  matrix products: 31.3 us -> 0 us
  between operations: 14.3 us -> 0.69 us
    psum x2 -> x0, waiting for transfers between devices: 554 us -> none  [the longest x1 450 us: per_device(): lax.psum((grad_first, grad_first_bias, grad_mid, grad_mid_bias, grad_last...]
    psum x1 -> x0, blocking collectives: 163 us -> none  [per_device(): lax.psum((grad_first, grad_first_bias, grad_mid, grad_mid_bias, grad_last...]
    all_gather x2 -> x0, waiting for transfers between devices: 159 us -> none  [the longest x1 84.6 us: per_device(): strip_all = lax.all_gather(strips_out, 'tile', axis=0, tiled=True)]
    pallas_call x0 -> x4, Pallas kernels: none -> 81.9 us  [the longest x1 32.4 us: exchange(): pl.pallas_call(exchange_kernel, out_shape=(jax.ShapeDtypeStruct((2, 2, 4,...]
    gather x16 -> x0, local copies, waits for them, and re-layouts: 63.2 us -> none  [choose_strip(): strips = strip_table[jnp.minimum(owner_ids, table_size - 1), strip_id]]
    reshape x4 -> x1, local copies, waits for them, and re-layouts: 31.8 us -> 0.13 us  [per_device(): wb_own = mid_weight.transpose(3, 0, 1, 2).reshape(64, 1152)]
    dot_general x10 -> x0, matrix products: 31.3 us -> none  [the longest x4 13.9 us: matmul_rows(): lax.dot_general(left_mat, right_mat, (((0,), (0,)), ((), ())), preferred_...]
    concatenate x10 -> x0, local copies, waits for them, and re-layouts: 30.4 us -> none  [patch_cols(): jnp.concatenate([padded_in[:, row_off:row_off + extent, col_off:col_off +...]
  transfers between devices with their start and end apart: 5 -> 0, of which waited for: 5 -> 0; matrix products, arithmetic and copies ran while one was open for 2% -> 0% of each run, Pallas kernels for 0% -> 0%
where the time goes in v1:
time: 95.7 us; the launch traced here: 95.3 us
  Pallas kernels  81.9 us (86%)
  local copies, waits for them, and re-layouts  11.4 us (12%)
  other arithmetic  1.24 us (1%)
    pallas_call x1, Pallas kernels, exchange(): pl.pallas_call(exchange_kernel, out_shape=(jax.ShapeDtypeStruct((2, 2, 4,...  32.4 us
    pallas_call x1, Pallas kernels, reduce_gradients(): pl.pallas_call(reduce_kernel, out_shape=jax.ShapeDtypeStruct((ROWS, 128),...  24.7 us
    pallas_call x1, Pallas kernels, compute(): pl.pallas_call(kernel, grid_spec=grid_spec, out_shape=(jax.ShapeDtypeStru...  24 us
    unnamed x22, local copies, waits for them, and re-layouts  9.47 us

profile of v1, /device:TPU:1, one launch (start us, length us, event | category | flops | bytes accessed | tf_op | source)
XLA Modules:
  0.0 95.3 jit_solution(4702351181879072031)
XLA Ops:
  0.6 0.8 fusion.1
  1.4 1.2 %fusion.refs_9_ = f32[1,128]{1,0:T(1,128)} fusion(f32[128]{0:T(128)} %param.16, pred[]{:T(512)S(6)} %eq.3, f32[64]{0:T(128)S(1)} %get-tuple-element.51, f32[64]{0:T(128)S(1)} %get-tuple-element.50), kind=kLoop, calls=%fused_computation.1 | loop fusion | flops 256 | bytes 1537 | tf_op jit(solution)/shard_map/reshape | solution.py:779
  2.7 1.0 %copy.21 = bf16[64,3,3,128]{3,2,1,0:T(4,128)(2,1)S(1)} copy(bf16[64,3,3,128]{3,0,2,1:T(8,128)(2,1)} %bitcast.14) | data formatting | bytes 294912 | tf_op jit(solution)/shard_map/transpose | solution.py:777
  3.7 0.1 reshape.52.wb_own.refs_7_
  3.9 0.0 copy-start
  3.9 1.6 %copy-done = bf16[4,32,32,256]{3,2,1,0:T(8,128)(2,1)S(1)} copy-done((bf16[4,32,32,256]{3,2,1,0:T(8,128)(2,1)S(1)}, bf16[4,32,32,256]{3,2,1,0:T(8,128)(2,1)}, u32[]{:S(2)}) %copy-start) | copy-done | bytes 2097176
  5.5 0.0 copy-start.3
  5.5 0.9 copy-done.3
  6.4 0.0 copy-start.5
  6.4 0.8 copy-done.5
  7.2 0.0 copy-start.9
  7.2 0.7 copy-done.9
  7.9 0.0 copy-start.1
  7.9 32.4 %shard_map.161 = (bf16[2,2,4,80,128]{4,3,2,1,0:T(8,128)(2,1)S(1)}, bf16[64,1152]{1,0:T(8,128)(2,1)S(1)}, bf16[64,512]{1,0:T(8,128)(2,1)S(1)}, bf16[128,512]{1,0:T(8,128)(2,1)S(1)}) custom-call(bf16[4,32,32,256]{3,2,1,0:T(8,128)(2,1)S(1)} %copy-done, s32[4,8]{1,0:T(4,128)S(1)} %copy-done.9, bf16[64,1152]{1,0:T(8,128)(2,1)S(1)} %reshape.52.wb_own.refs_7_, ...), custom_call_target="tpu_custom_call" | custom-call | tf_op jit(solution)/shard_map/pallas_call | solution.py:268
  40.2 0.0 copy-start.4
  40.2 0.7 copy-done.4
  41.0 0.0 copy-start.6
  41.0 0.7 copy-done.6
  41.6 0.0 copy-start.7
  41.7 0.7 copy-done.7
  42.3 0.0 copy-start.8
  42.3 0.6 copy-done.8
  42.9 0.0 copy-done.1
  42.9 24.0 %shard_map.162 = (bf16[4096,512]{1,0:T(8,128)(2,1)}, bf16[2,1536,128]{2,1,0:T(8,128)(2,1)}) custom-call(s32[1]{0:T(128)} %bitcast.refs_0_.ch_s, s32[4,8]{1,0:T(4,128)} %refs_1_.1, bf16[4096,256]{1,0:T(8,128)(2,1)} %bitcast.12, bf16[4096,512]{1,0:T(8,128)(2,1)} %bitcast.13, bf16[2,2,4,80,128]{4,3,2,1,0:T(8,128)(2,1)} %copy-done.4, bf16[256,128]{1,0:T(8,128)(2,1)} %refs_5_.1, ...), custom_call_target="tpu_custom_call" | custom-call | tf_op jit(solution)/shard_map/pallas_call | solution.py:595
  67.0 0.0 copy-start.2
  67.0 1.1 %copy-done.2 = bf16[2,1536,128]{2,1,0:T(8,128)(2,1)S(1)} copy-done((bf16[2,1536,128]{2,1,0:T(8,128)(2,1)S(1)}, bf16[2,1536,128]{2,1,0:T(8,128)(2,1)}, u32[]{:S(2)}) %copy-start.2) | copy-done | bytes 786456
  68.1 24.7 %shard_map.163.total = bf16[1536,128]{1,0:T(8,128)(2,1)S(1)} custom-call(bf16[2,1536,128]{2,1,0:T(8,128)(2,1)S(1)} %copy-done.2), custom_call_target="tpu_custom_call" | custom-call | tf_op jit(solution)/shard_map/pallas_call | solution.py:701
  92.8 0.9 shard_map.164
  93.7 0.7 copy.22
  94.4 0.9 copy.23
Async XLA Ops:
  3.9 1.6 %copy-start = (bf16[4,32,32,256]{3,2,1,0:T(8,128)(2,1)S(1)}, bf16[4,32,32,256]{3,2,1,0:T(8,128)(2,1)}, u32[]{:S(2)}) copy-start(bf16[4,32,32,256]{3,2,1,0:T(8,128)(2,1)} %feat.1) | copy-start | bytes 6291460
  5.5 0.9 copy-start.3
  6.4 0.8 copy-start.5
  7.2 0.7 copy-start.9
  7.9 35.1 %copy-start.1 = (bf16[64,1152]{1,0:T(8,128)(2,1)}, bf16[64,1152]{1,0:T(8,128)(2,1)S(1)}, u32[]{:S(2)}) copy-start(bf16[64,1152]{1,0:T(8,128)(2,1)S(1)} %reshape.52.wb_own.refs_7_) | copy-start | bytes 442372
  40.2 0.7 copy-start.4
  41.0 0.7 copy-start.6
  41.6 0.7 copy-start.7
  42.3 0.6 copy-start.8
  67.0 1.1 %copy-start.2 = (bf16[2,1536,128]{2,1,0:T(8,128)(2,1)S(1)}, bf16[2,1536,128]{2,1,0:T(8,128)(2,1)}, u32[]{:S(2)}) copy-start(bf16[2,1536,128]{2,1,0:T(8,128)(2,1)} %get-tuple-element.26.grads) | copy-start | bytes 2359300

commit v2 on v0

v2 whole, which is shorter than its diff:
```python
import math

import jax
import jax.numpy as jnp
from jax import lax
from jax.experimental import pallas as pl
from jax.experimental.pallas import tpu as pltpu
from jax.sharding import PartitionSpec as P

BF = jnp.bfloat16
F32 = jnp.float32
MESH = pl.DeviceIdType.MESH

ROW_FIRST = 0
ROW_MID = 128
ROW_LAST = 704
ROW_SIDE = 960
ROW_BIAS = 1472
ROWS = 1536
CORE_ROWS = ROWS // 2
PIECE = CORE_ROWS // 16

CHUNK = 512
PARTS = 8


def place():
    tile = lax.axis_index("tile")
    ch = lax.axis_index("ch")
    return tile // 16, (tile // 8) % 2, (tile // 2) % 4, tile % 2, ch


def device(y, zh, x, core, ch):
    return (((y * 2 + zh) * 4 + x) * 2 + core, ch)


def sigmoid(v):
    return 0.5 + 0.5 * jnp.tanh(0.5 * v)


def dot(a, b):
    return jnp.dot(a, b, preferred_element_type=F32)


def dot_nt(a, b):
    return lax.dot_general(a, b, (((1,), (1,)), ((), ())), preferred_element_type=F32)


def dot_tn(a, b):
    return lax.dot_general(a, b, (((0,), (0,)), ((), ())), preferred_element_type=F32)


def block_kernel(
    scale,
    features,
    cotangent,
    neighbours,
    w1_h,
    b1_h,
    wm_h,
    mid_bias_h,
    wl_h,
    ws_h,
    last_bias_h,
    output,
    total,
    feat,
    cot,
    near,
    near_s,
    w1,
    b1,
    wm,
    mid_bias_n,
    wl_part,
    ws_part,
    last_bias,
    wide,
    edges,
    table,
    table_out,
    table_s,
    every,
    pack,
    got,
    piece,
    halo,
    mid_bias,
    wf,
    wbt,
    wl,
    ws,
    first_pre,
    rim_pre,
    padded,
    patches,
    mid_delta,
    spread,
    rim,
    out,
    g_first,
    g_mid,
    g_last,
    g_side,
    g_first_bias,
    g_mid_bias,
    g_last_bias,
    grads,
    from_core,
    by_piece,
    from_plane,
    mine,
    from_z,
    done,
    local_sem,
    out_sem,
    send_sem,
    recv_sem,
    sum_send_sem,
    sum_recv_sem,
):
    y, zh, x, core, ch = place()
    row_role = core == 0
    along = jnp.where(row_role, x, y)
    across = jnp.where(row_role, y, x)
    own_place = y * 4 + x

    def gather_peer(step):
        to = lax.rem(along + step, 4)
        return device(jnp.where(row_role, y, to), zh, jnp.where(row_role, to, x), core, ch)

    def select_peer(step):
        to = lax.rem(across + step, 4)
        return device(jnp.where(row_role, to, y), zh, jnp.where(row_role, x, to), core, ch)

    def plane_peer(step):
        to = lax.rem(own_place + step, 16)
        return device(to // 4, zh, to % 4, core, ch)

    sibling = device(y, zh, x, 1 - core, ch)
    z_peers = [device(y, 1 - zh, x, role, 1 - ch) for role in (0, 1)]
    ch_same = device(y, zh, x, core, 1 - ch)
    ch_cross = device(y, zh, x, 1 - core, 1 - ch)
    z_even = device(y, 1 - zh, x, core, ch)
    z_odd = device(y, 1 - zh, x, core, 1 - ch)

    barrier = pltpu.get_barrier_semaphore()
    greeted = [sibling, *z_peers, ch_same, ch_cross, z_even]
    greeted += [plane_peer(step) for step in range(1, 16)]
    for peer in greeted:
        pl.semaphore_signal(barrier, inc=1, device_id=peer, device_id_type=MESH)

    loads = [
        (neighbours, near),
        (neighbours, near_s),
        *[(features.at[tile], feat.at[tile]) for tile in range(4)],
        (w1_h, w1),
        (b1_h, b1),
        (wm_h, wm.at[0]),
        (wl_h, wl_part.at[0]),
        (ws_h, ws_part.at[0]),
        (mid_bias_h, mid_bias_n),
        (last_bias_h, last_bias),
    ]
    loads += [
        (cotangent.at[pl.ds(pl.multiple_of((2 * ch + k) * 1024, 1024), 1024)], cot.at[k])
        for k in range(2)
    ]
    loading = []
    for number, (source, target) in enumerate(loads):
        made = pltpu.make_async_copy(source, target, local_sem.at[number])
        made.start()
        loading.append(made)

    loading[0].wait()
    ids = jnp.minimum(near[...], 255)
    in_y, in_zh, in_x, low = ids >> 6, (ids >> 5) & 1, (ids >> 3) & 3, ids & 7
    by_row = in_zh * 32 + in_x * 8 + low + 64 * in_y
    by_col = in_zh * 32 + in_y * 8 + low + 64 * in_x
    role = jnp.zeros_like(ids) + core
    table[across, core] = jnp.zeros((8, 128), jnp.int32)
    table[across, core, 0:4, 0:8] = jnp.where(role == 0, by_row, by_col)
    table_out[...] = jnp.zeros((8, 128), jnp.int32)
    table_out[0:4, 0:8] = jnp.where(role == 0, by_col, by_row)

    for tile in range(4):
        loading[2 + tile].wait()
        first_row = feat[tile, 0]
        last_row = feat[tile, 31]
        for half in range(2):
            lanes = slice(half * 128, half * 128 + 128)
            wide[0:512, :] = feat[tile, :, 0:16, lanes].astype(F32).reshape(512, 128)
            wide[512:1024, :] = feat[tile, :, 16:32, lanes].astype(F32).reshape(512, 128)
            edges[0, half, tile, 0] = first_row[:, lanes]
            edges[0, half, tile, 1] = last_row[:, lanes]
            edges[1, half, tile, 0] = wide[pl.ds(0, 32, stride=16), :].astype(BF)
            edges[1, half, tile, 1] = wide[pl.ds(527, 32, stride=16), :].astype(BF)

    def block(plane, at):
        return pl.ds(pl.multiple_of(plane * 32 + at * 8, 8), 8)

    def part(plane, at, owner):
        return pl.ds(pl.multiple_of(plane * 32 + at * 8 + owner * 4, 4), 4)

    every[part(zh, along, core)] = edges[core, ch]
    for number in (8, 9, 10):
        loading[number].wait()

    pl.semaphore_wait(barrier, len(greeted))

    sent = []

    def copy(number, source, target, peer, arrives):
        return pltpu.make_async_remote_copy(
            src_ref=source,
            dst_ref=target,
            send_sem=send_sem.at[number],
            recv_sem=recv_sem.at[arrives],
            device_id=peer,
            device_id_type=MESH,
        )

    def start(number, source, target, peer, arrives):
        made = copy(number, source, target, peer, arrives)
        made.start()
        sent.append(made)

    def arrived(number, target):
        copy(0, target, target, sibling, number).wait_recv()

    def first_layer(tile):
        pre = dot(feat[tile].reshape(1024, 256), w1[...]) + b1[...]
        first_pre[tile] = pre
        act = pre * sigmoid(pre)
        padded[tile, 1:33, 8:40, :] = act.reshape(32, 32, 128)

    start(1, edges.at[1 - core, ch], every.at[part(zh, across, core)], sibling, 1)
    for k in range(2):
        start(
            2 + k,
            edges.at[k, 1 - ch],
            every.at[part(zh, x if k == 0 else y, core)],
            z_peers[k],
            2 + core,
        )
    start(0, table_out, table.at[along, core], sibling, 0)
    start(4, wm.at[0], wm.at[1], ch_same, 4)
    start(5, wl_part.at[0], wl_part.at[1], ch_same, 5)
    start(6, ws_part.at[0], ws_part.at[1], ch_same, 6)
    loading[6].wait()
    loading[7].wait()
    first_layer(0)

    arrived(1, every.at[part(zh, along, 1 - core)])
    own_block = every.at[block(zh, along)]
    start(7, own_block, own_block, gather_peer(1), 7)
    start(8, own_block, own_block, gather_peer(3), 8)
    arrived(0, table.at[across, 1 - core])
    for step in range(1, 4):
        start(8 + step, table.at[across], table.at[across], select_peer(step), 8 + step)
    arrived(2, every.at[part(1 - zh, along, 0)])
    arrived(3, every.at[part(1 - zh, along, 1)])
    far_block = every.at[block(1 - zh, along)]
    start(12, far_block, far_block, gather_peer(1), 12)
    start(13, far_block, far_block, gather_peer(3), 13)
    first_layer(1)
    before = lax.rem(along + 3, 4)
    after = lax.rem(along + 1, 4)
    opposite = lax.rem(along + 2, 4)
    for plane, first, second in ((zh, 7, 14), (1 - zh, 12, 16)):
        arrived(first, every.at[block(plane, before)])
        passed = every.at[part(plane, before, 0)]
        start(second, passed, passed, gather_peer(1), second)
        arrived(first + 1, every.at[block(plane, after)])
        passed = every.at[part(plane, after, 1)]
        start(second + 1, passed, passed, gather_peer(3), second + 1)
    for step in range(1, 4):
        arrived(8 + step, table.at[lax.rem(across + 4 - step, 4)])
    to_scalars = pltpu.make_async_copy(table, table_s, local_sem.at[len(loads)])
    to_scalars.start()
    first_layer(2)
    to_scalars.wait()
    for second, plane in ((14, zh), (16, 1 - zh)):
        arrived(second, every.at[part(plane, opposite, 0)])
        arrived(second + 1, every.at[part(plane, opposite, 1)])

    first_dir = 1 + 2 * core
    second_dir = 6 - 2 * core
    rows16 = lax.broadcasted_iota(jnp.int32, (16, 128), 0)

    for step in (2, 1, 3, 0):
        wanted = lax.rem(across + step, 4)
        into = pack.at[step] if step else got.at[0]

        def pack_tile(number, carry, wanted=wanted, into=into):
            owner, tile = number // 4, number % 4

            def held(d):
                return table_s[wanted, owner, tile, d] & 63

            into[owner, tile, 0:32, :] = every[held(first_dir), 1]
            into[owner, tile, 32:64, :] = every[held(second_dir), 0]
            corners = jnp.zeros((16, 128), F32)
            for k, (d, which, at) in enumerate(((0, 1, 31), (2, 1, 0), (5, 0, 31), (7, 0, 0))):
                near_rows = every[held(d), which, 16 * (at // 16) : 16 * (at // 16) + 16, :]
                near_rows = near_rows.astype(F32)[at % 16 : at % 16 + 1]
                corners = jnp.where(rows16 == k, near_rows, corners)
            into[owner, tile, 64:80, :] = corners.astype(BF)
            return carry

        lax.fori_loop(0, 8, pack_tile, 0)
        if step:
            start(17 + step, pack.at[step], got.at[step], select_peer(step), 17 + step)
    first_layer(3)
    for step in range(1, 4):
        arrived(17 + step, got.at[step])

    def finish_tile(owner, tile):
        def chosen(d, rows):
            from_step = (across + 4 - (table_s[across, owner, tile, d] >> 6)) & 3
            return got[from_step, owner, tile, rows, :]

        piece[owner, tile, 0:32, :] = chosen(first_dir, slice(0, 32))
        piece[owner, tile, 32:64, :] = chosen(second_dir, slice(32, 64))
        corners = jnp.zeros((16, 128), F32)
        for k, d in enumerate((0, 2, 5, 7)):
            corners = jnp.where(rows16 == k, chosen(d, slice(64, 80)).astype(F32), corners)
        piece[owner, tile, 64:80, :] = corners.astype(BF)

    for owner, copies in (
        (1 - core, ((23, ch_cross), (21, sibling))),
        (core, ((22, ch_same),)),
    ):
        lax.fori_loop(0, 4, lambda tile, c, owner=owner: (finish_tile(owner, tile), c)[1], 0)
        for number, peer in copies:
            start(number, piece.at[owner], halo.at[core, ch], peer, number)
    halo[core, ch] = piece[core]

    arrived(4, wm.at[1])
    arrived(5, wl_part.at[1])
    arrived(6, ws_part.at[1])
    for number in (11, 12):
        loading[number].wait()
    for i in range(3):
        for half in range(2):
            at = i * 128 + half * 64
            for j in range(3):
                source = (i * 3 + j) * 64
                wbt[at : at + 64, j * 128 : j * 128 + 128] = wm[half, source : source + 64, :]
        wf[i] = wbt[i * 128 : i * 128 + 128, :].astype(F32).T.astype(BF)
    own128 = pl.multiple_of(ch * 128, 128)
    other128 = pl.multiple_of((1 - ch) * 128, 128)
    wl[0:64, :] = wl_part[0]
    wl[64:128, :] = wl_part[1]
    ws[pl.ds(own128, 128), :] = ws_part[0]
    ws[pl.ds(other128, 128), :] = ws_part[1]
    bias = mid_bias_n[...]
    swapped = jnp.concatenate([bias[:, 64:128], bias[:, 0:64]], axis=1)
    mid_bias[...] = jnp.where(ch == 0, bias, swapped)
    for ref in (g_first, g_mid, g_last, g_side, g_first_bias, g_mid_bias, g_last_bias):
        ref[...] = jnp.zeros_like(ref)
    blank = jnp.zeros((32, 128), BF)
    for line, lanes in ((32, 0), (33, 0), (0, 128), (33, 128), (0, 256), (1, 256)):
        mid_delta[line, :, lanes : lanes + 128] = blank

    loading[1].wait()
    arrived(21, halo.at[1 - core, ch])
    arrived(22, halo.at[core, 1 - ch])
    arrived(23, halo.at[1 - core, 1 - ch])


    def here(tile, direction):
        return jnp.where(near_s[tile, direction] < 256, 1.0, 0.0).astype(F32)

    def rim_features(tile):
        return jnp.concatenate(
            [
                jnp.concatenate([halo[0, 0, tile], halo[0, 1, tile]], axis=1),
                jnp.concatenate([halo[1, 0, tile], halo[1, 1, tile]], axis=1),
            ],
            axis=0,
        )

    def pad(tile):
        pre = dot(rim_features(tile), w1[...]) + b1[...]
        rim_pre[...] = pre
        act = pre * sigmoid(pre)
        rim[...] = act
        padded[tile, 0, 8:40, :] = act[0:32] * here(tile, 1)
        padded[tile, 33, 8:40, :] = act[32:64] * here(tile, 6)
        padded[tile, 1:33, 7:8, :] = (act[80:112] * here(tile, 3)).reshape(32, 1, 128)
        padded[tile, 1:33, 40:41, :] = (act[112:144] * here(tile, 4)).reshape(32, 1, 128)
        padded[tile, 0, 7:8, :] = rim[64:65, :] * here(tile, 0)
        padded[tile, 0, 40:41, :] = rim[65:66, :] * here(tile, 2)
        padded[tile, 33, 7:8, :] = rim[66:67, :] * here(tile, 5)
        padded[tile, 33, 40:41, :] = rim[67:68, :] * here(tile, 7)
        for j in range(3):
            patches[:, :, j * 128 : j * 128 + 128] = padded[tile, :, 7 + j : 39 + j, :].astype(BF)

    high = CHUNK // 32

    def forward(tile, number):
        row = pl.multiple_of(number * CHUNK, CHUNK)
        line = number * high
        views = [patches[pl.ds(line + i, high)].reshape(CHUNK, 384) for i in range(3)]
        mid_pre = mid_bias[...] + dot(views[0], wf[0]) + dot(views[1], wf[1]) + dot(views[2], wf[2])
        mid_sig = sigmoid(mid_pre)
        mid_val = mid_pre * mid_sig
        mid_act = mid_val.astype(BF)
        x_part = feat[tile, pl.ds(line, high)].reshape(CHUNK, 256)
        out_pre = dot(mid_act, wl[...]) + dot(x_part, ws[...]) + last_bias[...]
        sig = sigmoid(out_pre)
        val = out_pre * sig
        out[tile, pl.ds(row, CHUNK), :] = val.astype(BF)
        return row, line, views, mid_sig, mid_val, mid_act, x_part, sig, val

    def write_out(tile, number):
        return pltpu.make_async_copy(out.at[tile], output.at[tile], out_sem.at[number])

    def forward_tile(tile, first, last):
        def body(number, carry):
            forward(tile, number)
            return carry

        lax.fori_loop(first, last, body, 0, unroll=True)

    def whole_tile(k, carry):
        tile = 2 * ch + k
        pad(tile)

        def body(number, inner):
            row, line, views, mid_sig, mid_val, mid_act, x_part, sig, val = forward(tile, number)
            slope = sig + val * (1.0 - sig)
            grad_out = (cot[k, pl.ds(row, CHUNK), :].astype(F32) * scale * slope).astype(BF)
            g_last[...] += dot_tn(mid_act, grad_out)
            g_side[...] += dot_tn(x_part, grad_out)
            g_last_bias[...] += grad_out.astype(F32).reshape(CHUNK // 8, 8, 512).sum(axis=0)
            mid_back = dot_nt(grad_out, wl[...])
            delta = (mid_back * (mid_sig + mid_val * (1.0 - mid_sig))).astype(BF)
            g_mid_bias[...] += delta.astype(F32).reshape(CHUNK // 8, 8, 128).sum(axis=0)
            for i in range(3):
                g_mid[i] += dot_tn(delta, views[i])
            for i in range(3):
                mid_delta[pl.ds(line + i, high), :, i * 128 : i * 128 + 128] = delta.reshape(
                    high, 32, 128
                )
            return inner

        lax.fori_loop(0, 1024 // CHUNK, body, 0, unroll=True)
        write_out(tile, k).start()

        back = dot(mid_delta[...].reshape(1088, 384), wbt[...]).reshape(34, 32, 384)
        spread[:, 0:8, :] = jnp.zeros((34, 8, 128), F32)
        spread[:, 40:48, :] = jnp.zeros((34, 8, 128), F32)
        spread[:, 8:40, :] = back[:, :, 128:256]
        spread[:, 7:39, :] += back[:, :, 0:128]
        spread[:, 9:41, :] += back[:, :, 256:384]

        pre = first_pre[tile]
        sig = sigmoid(pre)
        slope = sig + pre * sig * (1.0 - sig)
        delta = (spread[1:33, 8:40, :].reshape(1024, 128) * slope).astype(BF)
        rim[...] = jnp.zeros_like(rim)
        rim[0:32, :] = spread[0, 8:40, :] * here(tile, 1)
        rim[32:64, :] = spread[33, 8:40, :] * here(tile, 6)
        rim[64:65, :] = spread[0, 7:8, :] * here(tile, 0)
        rim[65:66, :] = spread[0, 40:41, :] * here(tile, 2)
        rim[66:67, :] = spread[33, 7:8, :] * here(tile, 5)
        rim[67:68, :] = spread[33, 40:41, :] * here(tile, 7)
        rim[80:112, :] = spread[1:33, 7:8, :].reshape(32, 128) * here(tile, 3)
        rim[112:144, :] = spread[1:33, 40:41, :].reshape(32, 128) * here(tile, 4)
        pre = rim_pre[...]
        sig = sigmoid(pre)
        slope = sig + pre * sig * (1.0 - sig)
        delta_rim = (rim[...] * slope).astype(BF)
        g_first[...] += dot_tn(delta, feat[tile].reshape(1024, 256))
        g_first[...] += dot_tn(delta_rim, rim_features(tile))
        g_first_bias[...] += delta.astype(F32).reshape(128, 8, 128).sum(axis=0)
        g_first_bias[...] += delta_rim.astype(F32).reshape(20, 8, 128).sum(axis=0)
        return carry

    loading[13].wait()
    loading[14].wait()
    lax.fori_loop(0, 2, whole_tile, 0)


    bias_first = jnp.sum(g_first_bias[...], axis=0, keepdims=True)
    bias_mid = jnp.sum(g_mid_bias[...], axis=0, keepdims=True)
    bias_last = jnp.sum(g_last_bias[...], axis=0, keepdims=True)
    for half in range(2):
        whose = ch if half == 0 else 1 - ch
        start64 = pl.multiple_of(whose * 64, 64)
        start128 = pl.multiple_of(whose * 128, 128)
        order = slice(half * 64, half * 64 + 64)
        for k in range(2):
            at = ROW_FIRST + k * 64
            lanes = slice(k * 128, k * 128 + 128)
            grads[half, at : at + 64, :] = g_first[pl.ds(start64, 64), lanes].astype(BF)
        for i in range(3):
            for j in range(3):
                at = ROW_MID + (i * 3 + j) * 64
                lanes = slice(j * 128, j * 128 + 128)
                grads[half, at : at + 64, :] = g_mid[i, order, lanes].astype(BF)
        for k in range(4):
            lanes = slice(k * 128, k * 128 + 128)
            at = ROW_LAST + k * 64
            grads[half, at : at + 64, :] = g_last[order, lanes].astype(BF)
            at = ROW_SIDE + k * 128
            grads[half, at : at + 128, :] = g_side[pl.ds(start128, 128), lanes].astype(BF)
        mid_row = bias_mid
        if half == 1:
            mid_row = jnp.concatenate([bias_mid[:, 64:128], bias_mid[:, 0:64]], axis=1)
        rows = jnp.where(rows16 == 0, bias_first, jnp.where(rows16 == 1, mid_row, 0.0))
        for k in range(4):
            rows = jnp.where(rows16 == 2 + k, bias_last[:, k * 128 : k * 128 + 128], rows)
        grads[half, ROW_BIAS : ROW_BIAS + 16, :] = rows.astype(BF)
        grads[half, ROW_BIAS + 16 : ROWS, :] = jnp.zeros((ROWS - ROW_BIAS - 16, 128), BF)


    def hand(number, source, target, peer):
        made = pltpu.make_async_remote_copy(
            src_ref=source,
            dst_ref=target,
            send_sem=sum_send_sem.at[number],
            recv_sem=sum_recv_sem.at[number],
            device_id=peer,
            device_id_type=MESH,
        )
        made.start()
        sent.append(made)
        return made

    third = lax.rem(2 + 2 * ch, 4)
    fourth = lax.rem(3 + 2 * ch, 4)
    count = 1024 // CHUNK

    own_rows = pl.multiple_of(core * CORE_ROWS, CORE_ROWS)
    other_rows = pl.multiple_of((1 - core) * CORE_ROWS, CORE_ROWS)
    swap = hand(0, grads.at[:, pl.ds(other_rows, CORE_ROWS)], from_core, sibling)
    pad(third)
    swap.wait_recv()
    for half in range(2):
        added = grads[half, pl.ds(own_rows, CORE_ROWS), :].astype(F32) + from_core[half].astype(F32)
        by_piece[:, half] = added.astype(BF).reshape(16, PIECE, 128)
    plane = []
    for step in range(1, 16):
        to = lax.rem(own_place + step, 16)
        plane.append(hand(step, by_piece.at[to], from_plane.at[step], plane_peer(step)))
    forward_tile(third, 0, count)
    write_out(third, 2).start()
    added = by_piece[own_place].astype(F32)
    for step, made in enumerate(plane, 1):
        made.wait_recv()
        added = added + from_plane[step].astype(F32)
    mine[...] = added.astype(BF)
    hops = []
    for k, (half, peer) in enumerate(((0, z_even), (1, ch_same), (1, z_odd))):
        hops.append(hand(16 + k, mine.at[half], from_z.at[k], peer))
    pad(fourth)
    forward_tile(fourth, 0, count // 2)
    added = added[0]
    for k, made in enumerate(hops):
        made.wait_recv()
        added = added + from_z[k].astype(F32)
    at = pl.multiple_of(own_rows + own_place * PIECE, 16)
    done[pl.ds(at, PIECE), :] = added.astype(BF)
    backs = []
    for step in range(1, 16):
        here_too = done.at[pl.ds(at, PIECE)]
        backs.append(hand(18 + step, here_too, here_too, plane_peer(step)))
    forward_tile(fourth, count // 2, count)
    write_out(fourth, 3).start()
    for made in backs:
        made.wait_recv()
    half_sum = done.at[pl.ds(own_rows, CORE_ROWS)]
    last = hand(34, half_sum, half_sum, sibling)
    last.wait_recv()
    whole_sum = pltpu.make_async_copy(done, total, out_sem.at[4])
    whole_sum.start()
    for made in sent:
        made.wait_send()
    for number, tile in enumerate((2 * ch, 2 * ch + 1, third, fourth)):
        write_out(tile, number).wait()
    whole_sum.wait()


def block(
    features,
    cotangent,
    neighbours,
    w1,
    b1,
    wm,
    mid_bias,
    wl,
    ws,
    last_bias,
):
    scale = 1.0 / math.sqrt(4096)
    anywhere = pl.BlockSpec(memory_space=pl.ANY)

    def kernel(*refs):
        block_kernel(scale, *refs)

    return pl.pallas_call(
        kernel,
        in_specs=[anywhere] * 10,
        out_specs=(anywhere, anywhere),
        out_shape=(
            jax.ShapeDtypeStruct((4, 1024, 512), BF),
            jax.ShapeDtypeStruct((ROWS, 128), BF),
        ),
        scratch_shapes=[
            pltpu.VMEM((4, 32, 32, 256), BF),
            pltpu.VMEM((2, 1024, 512), BF),
            pltpu.VMEM((4, 8), jnp.int32),
            pltpu.SMEM((4, 8), jnp.int32),
            pltpu.VMEM((256, 128), BF),
            pltpu.VMEM((1, 128), F32),
            pltpu.VMEM((2, 576, 128), BF),
            pltpu.VMEM((1, 128), F32),
            pltpu.VMEM((2, 64, 512), BF),
            pltpu.VMEM((2, 128, 512), BF),
            pltpu.VMEM((1, 512), F32),
            pltpu.VMEM((1024, 128), F32),
            pltpu.VMEM((2, 2, 4, 2, 32, 128), BF),
            pltpu.VMEM((4, 2, 8, 128), jnp.int32),
            pltpu.VMEM((8, 128), jnp.int32),
            pltpu.SMEM((4, 2, 8, 128), jnp.int32),
            pltpu.VMEM((64, 2, 32, 128), BF),
            pltpu.VMEM((4, 2, 4, 80, 128), BF),
            pltpu.VMEM((4, 2, 4, 80, 128), BF),
            pltpu.VMEM((2, 4, 80, 128), BF),
            pltpu.VMEM((2, 2, 4, 80, 128), BF),
            pltpu.VMEM((1, 128), F32),
            pltpu.VMEM((3, 384, 128), BF),
            pltpu.VMEM((384, 384), BF),
            pltpu.VMEM((128, 512), BF),
            pltpu.VMEM((256, 512), BF),
            pltpu.VMEM((4, 1024, 128), F32),
            pltpu.VMEM((160, 128), F32),
            pltpu.VMEM((4, 34, 48, 128), F32),
            pltpu.VMEM((34, 32, 384), BF),
            pltpu.VMEM((34, 32, 384), BF),
            pltpu.VMEM((34, 48, 128), F32),
            pltpu.VMEM((160, 128), F32),
            pltpu.VMEM((4, 1024, 512), BF),
            pltpu.VMEM((128, 256), F32),
            pltpu.VMEM((3, 128, 384), F32),
            pltpu.VMEM((128, 512), F32),
            pltpu.VMEM((256, 512), F32),
            pltpu.VMEM((8, 128), F32),
            pltpu.VMEM((8, 128), F32),
            pltpu.VMEM((8, 512), F32),
            pltpu.VMEM((2, ROWS, 128), BF),
            pltpu.VMEM((2, CORE_ROWS, 128), BF),
            pltpu.VMEM((16, 2, PIECE, 128), BF),
            pltpu.VMEM((16, 2, PIECE, 128), BF),
            pltpu.VMEM((2, PIECE, 128), BF),
            pltpu.VMEM((3, PIECE, 128), BF),
            pltpu.VMEM((ROWS, 128), BF),
            pltpu.SemaphoreType.DMA((16,)),
            pltpu.SemaphoreType.DMA((5,)),
            pltpu.SemaphoreType.DMA((24,)),
            pltpu.SemaphoreType.DMA((24,)),
            pltpu.SemaphoreType.DMA((35,)),
            pltpu.SemaphoreType.DMA((35,)),
        ],
        compiler_params=pltpu.CompilerParams(
            collective_id=0, has_side_effects=True, vmem_limit_bytes=60 * 2**20
        ),
    )(features, cotangent, neighbours, w1, b1, wm, mid_bias, wl, ws, last_bias)


def finish_kernel(
    out,
    total_h,
    output,
    g_first,
    g_first_bias,
    g_mid,
    g_mid_bias,
    g_last,
    g_side,
    g_last_bias,
    total,
    staged,
    in_sem,
    out_sem,
):
    loading = pltpu.make_async_copy(total_h, total, in_sem.at[PARTS])
    loading.start()
    reads, writes = [], []
    for k in range(PARTS):
        reads.append(pltpu.make_async_copy(out.at[k], staged.at[k], in_sem.at[k]))
        writes.append(pltpu.make_async_copy(staged.at[k], output.at[k], out_sem.at[k]))
        reads[k].start()
    for k in range(PARTS):
        reads[k].wait()
        writes[k].start()
    loading.wait()

    def rows(at, count):
        return total[at : at + count, :].astype(F32)

    for k in range(2):
        g_first[:, k * 128 : k * 128 + 128] = rows(ROW_FIRST + k * 64, 64)
    for k in range(9):
        g_mid[k // 3, k % 3] = rows(ROW_MID + k * 64, 64)
    bias = rows(ROW_BIAS, 16)
    for k in range(4):
        lanes = slice(k * 128, k * 128 + 128)
        g_last[:, lanes] = rows(ROW_LAST + k * 64, 64)
        g_side[:, lanes] = rows(ROW_SIDE + k * 128, 128)
        g_last_bias[:, lanes] = bias[2 + k : 3 + k, :]
    ch = lax.axis_index("ch")
    g_first_bias[...] = jnp.where(ch == 0, bias[0:1, 0:64], bias[0:1, 64:128])
    g_mid_bias[...] = bias[1:2, 0:64]
    for made in writes:
        made.wait()


def finish(out, total):
    vmem = pl.BlockSpec(memory_space=pltpu.VMEM)
    return pl.pallas_call(
        finish_kernel,
        in_specs=[pl.BlockSpec(memory_space=pl.ANY)] * 2,
        out_specs=(pl.BlockSpec(memory_space=pl.ANY), *[vmem] * 7),
        out_shape=(
            jax.ShapeDtypeStruct(out.shape, BF),
            *[
                jax.ShapeDtypeStruct(shape, F32)
                for shape in (
                    (64, 256),
                    (1, 64),
                    (3, 3, 64, 128),
                    (1, 64),
                    (64, 512),
                    (128, 512),
                    (1, 512),
                )
            ],
        ),
        scratch_shapes=[
            pltpu.VMEM((ROWS, 128), BF),
            pltpu.VMEM(out.shape, BF),
            pltpu.SemaphoreType.DMA((PARTS + 1,)),
            pltpu.SemaphoreType.DMA((PARTS,)),
        ],
        compiler_params=pltpu.CompilerParams(vmem_limit_bytes=60 * 2**20),
    )(out, total)


def per_device(
    features,
    cotangent,
    neighbours,
    first_weight,
    first_bias,
    mid_weight,
    mid_bias,
    last_weight,
    side_weight,
    last_bias,
):
    out, total = block(
        features,
        cotangent.reshape(4096, 512),
        neighbours,
        first_weight,
        first_bias.reshape(1, 128),
        mid_weight.transpose(0, 1, 3, 2).reshape(576, 128),
        mid_bias.reshape(1, 128),
        last_weight,
        side_weight,
        last_bias.reshape(1, 512),
    )
    output, g_first, g_first_bias, g_mid, g_mid_bias, g_last, g_side, g_last_bias = finish(
        out.reshape(PARTS, 4096 // PARTS, 512), total
    )
    return (
        output.reshape(4, 32, 32, 512),
        g_first.T,
        g_first_bias.reshape(64),
        g_mid.transpose(0, 1, 3, 2),
        g_mid_bias.reshape(64),
        g_last,
        g_side,
        g_last_bias.reshape(512),
    )


def solution(mesh):
    return jax.shard_map(
        per_device,
        mesh=mesh,
        in_specs=(
            P("tile", None, None, None),
            P("tile", None, None, None),
            P("tile", None),
            P(),
            P(),
            P(None, None, None, "ch"),
            P(),
            P("ch", None),
            P("ch", None),
            P(),
        ),
        out_specs=(
            P("tile", None, None, None),
            P(None, "ch"),
            P("ch"),
            P(None, None, None, "ch"),
            P("ch"),
            P("ch", None),
            P("ch", None),
            P(),
        ),
        check_vma=False,
    )
```

time: 1170 us -> 67.7 us (0.06)
  waiting for transfers between devices: 731 us -> 0 us
  local copies, waits for them, and re-layouts: 188 us -> 0 us
  blocking collectives: 163 us -> 0 us
  Pallas kernels: 0 us -> 67 us
  other arithmetic: 33 us -> 0 us
  matrix products: 31.3 us -> 0 us
  between operations: 14.3 us -> 0.64 us
    psum x2 -> x0, waiting for transfers between devices: 554 us -> none  [the longest x1 450 us: per_device(): lax.psum((grad_first, grad_first_bias, grad_mid, grad_mid_bias, grad_last...]
    psum x1 -> x0, blocking collectives: 163 us -> none  [per_device(): lax.psum((grad_first, grad_first_bias, grad_mid, grad_mid_bias, grad_last...]
    all_gather x2 -> x0, waiting for transfers between devices: 159 us -> none  [the longest x1 84.6 us: per_device(): strip_all = lax.all_gather(strips_out, 'tile', axis=0, tiled=True)]
    pallas_call x0 -> x2, Pallas kernels: none -> 67 us  [the longest x1 62.4 us: block(): pl.pallas_call(kernel, in_specs=[anywhere] * 10, out_specs=(anywhere, any...]
    gather x16 -> x0, local copies, waits for them, and re-layouts: 63.2 us -> none  [choose_strip(): strips = strip_table[jnp.minimum(owner_ids, table_size - 1), strip_id]]
    unnamed x81 -> x0, local copies, waits for them, and re-layouts: 38.6 us -> none
    reshape x4 -> x0, local copies, waits for them, and re-layouts: 31.8 us -> none  [the longest x1 15.8 us: per_device(): strip_all = strip_all.reshape(all_tiles, 4, extent, full_mid)]
    dot_general x10 -> x0, matrix products: 31.3 us -> none  [the longest x4 13.9 us: matmul_rows(): lax.dot_general(left_mat, right_mat, (((0,), (0,)), ((), ())), preferred_...]
  transfers between devices with their start and end apart: 5 -> 0, of which waited for: 5 -> 0; matrix products, arithmetic and copies ran while one was open for 2% -> 0% of each run, Pallas kernels for 0% -> 0%
where the time goes in v2:
time: 67.7 us; the launch traced here: 67.6 us
  Pallas kernels  67 us (99%)
    pallas_call x1, Pallas kernels, block(): pl.pallas_call(kernel, in_specs=[anywhere] * 10, out_specs=(anywhere, any...  62.4 us
    pallas_call x1, Pallas kernels, finish(): pl.pallas_call(finish_kernel, in_specs=[pl.BlockSpec(memory_space=pl.ANY)...  4.58 us

profile of v2, /device:TPU:1, one launch (start us, length us, event | category | flops | bytes accessed | tf_op | source)
XLA Modules:
  0.0 67.6 jit_solution(7314439840758296388)
XLA Ops:
  0.6 62.4 %shard_map.161 = (bf16[4,1024,512]{2,1,0:T(8,128)(2,1)}, bf16[1536,128]{1,0:T(8,128)(2,1)}) custom-call(bf16[4,32,32,256]{3,2,1,0:T(8,128)(2,1)} %refs_0_.1, bf16[4096,512]{1,0:T(8,128)(2,1)} %bitcast.14, s32[4,8]{1,0:T(4,128)} %refs_2_.1, bf16[256,128]{1,0:T(8,128)(2,1)} %refs_3_.1, f32[1,128]{1,0:T(1,128)} %bitcast.18, bf16[576,128]{1,0:T(8,128)(2,1)} %bitcast.16, ...), custom_call_target="tpu_custom_call" | custom-call | tf_op jit(solution)/shard_map/pallas_call | solution.py:605
  63.0 4.6 %shard_map.162 = (bf16[8,512,512]{2,1,0:T(8,128)(2,1)}, f32[64,256]{1,0:T(8,128)}, f32[1,64]{1,0:T(1,128)}, f32[3,3,64,128]{3,2,1,0:T(8,128)}, f32[1,64]{1,0:T(1...) custom-call(bf16[8,512,512]{2,1,0:T(8,128)(2,1)} %bitcast.15, ...), custom_call_target="tpu_custom_call" | custom-call | tf_op jit(solution)/shard_map/pallas_call | solution.py:725

commit v3 on v2

--- a/solution.py
+++ b/solution.py
@@ -19,6 +19,9 @@
 ROWS = 1536
 CORE_ROWS = ROWS // 2
 PIECE = CORE_ROWS // 16
+
+CORNERS = ((0, 1, 31), (2, 1, 0), (5, 0, 31), (7, 0, 0))
+PLACES = ((0, 0, 7), (2, 0, 40), (5, 33, 7), (7, 33, 40))
 
 CHUNK = 512
 PARTS = 8
@@ -62,7 +65,7 @@
     wl_h,
     ws_h,
     last_bias_h,
-    output,
+    out,
     total,
     feat,
     cot,
@@ -82,7 +85,8 @@
     table_s,
     every,
     pack,
-    got,
+    got_first,
+    got_second,
     piece,
     halo,
     mid_bias,
@@ -97,7 +101,6 @@
     mid_delta,
     spread,
     rim,
-    out,
     g_first,
     g_mid,
     g_last,
@@ -113,7 +116,6 @@
     from_z,
     done,
     local_sem,
-    out_sem,
     send_sem,
     recv_sem,
     sum_send_sem,
@@ -196,9 +198,6 @@
             edges[1, half, tile, 0] = wide[pl.ds(0, 32, stride=16), :].astype(BF)
             edges[1, half, tile, 1] = wide[pl.ds(527, 32, stride=16), :].astype(BF)
 
-    def block(plane, at):
-        return pl.ds(pl.multiple_of(plane * 32 + at * 8, 8), 8)
-
     def part(plane, at, owner):
         return pl.ds(pl.multiple_of(plane * 32 + at * 8 + owner * 4, 4), 4)
 
@@ -243,6 +242,16 @@
             z_peers[k],
             2 + core,
         )
+    def ring_number(far, owner, back):
+        return 30 + far * 4 + owner * 2 + back
+
+    def ring(far, owner):
+        strips = every.at[part(1 - zh if far else zh, along, owner)]
+        for back, peer in ((0, gather_peer(1)), (1, gather_peer(3))):
+            number = ring_number(far, owner, back)
+            start(number, strips, strips, peer, number)
+
+    ring(0, core)
     start(0, table_out, table.at[along, core], sibling, 0)
     start(4, wm.at[0], wm.at[1], ch_same, 4)
     start(5, wl_part.at[0], wl_part.at[1], ch_same, 5)
@@ -252,90 +261,30 @@
     first_layer(0)
 
     arrived(1, every.at[part(zh, along, 1 - core)])
-    own_block = every.at[block(zh, along)]
-    start(7, own_block, own_block, gather_peer(1), 7)
-    start(8, own_block, own_block, gather_peer(3), 8)
+    ring(0, 1 - core)
     arrived(0, table.at[across, 1 - core])
     for step in range(1, 4):
         start(8 + step, table.at[across], table.at[across], select_peer(step), 8 + step)
-    arrived(2, every.at[part(1 - zh, along, 0)])
-    arrived(3, every.at[part(1 - zh, along, 1)])
-    far_block = every.at[block(1 - zh, along)]
-    start(12, far_block, far_block, gather_peer(1), 12)
-    start(13, far_block, far_block, gather_peer(3), 13)
+    for owner in range(2):
+        arrived(2 + owner, every.at[part(1 - zh, along, owner)])
+        ring(1, owner)
     first_layer(1)
     before = lax.rem(along + 3, 4)
     after = lax.rem(along + 1, 4)
     opposite = lax.rem(along + 2, 4)
-    for plane, first, second in ((zh, 7, 14), (1 - zh, 12, 16)):
-        arrived(first, every.at[block(plane, before)])
-        passed = every.at[part(plane, before, 0)]
-        start(second, passed, passed, gather_peer(1), second)
-        arrived(first + 1, every.at[block(plane, after)])
-        passed = every.at[part(plane, after, 1)]
-        start(second + 1, passed, passed, gather_peer(3), second + 1)
+    for far, plane in enumerate((zh, 1 - zh)):
+        for owner, back, origin, peer in (
+            (0, 0, before, gather_peer(1)),
+            (1, 1, after, gather_peer(3)),
+        ):
+            passed = every.at[part(plane, origin, owner)]
+            arrived(ring_number(far, owner, back), passed)
+            start(14 + far * 2 + owner, passed, passed, peer, 14 + far * 2 + owner)
     for step in range(1, 4):
         arrived(8 + step, table.at[lax.rem(across + 4 - step, 4)])
     to_scalars = pltpu.make_async_copy(table, table_s, local_sem.at[len(loads)])
     to_scalars.start()
     first_layer(2)
-    to_scalars.wait()
-    for second, plane in ((14, zh), (16, 1 - zh)):
-        arrived(second, every.at[part(plane, opposite, 0)])
-        arrived(second + 1, every.at[part(plane, opposite, 1)])
-
-    first_dir = 1 + 2 * core
-    second_dir = 6 - 2 * core
-    rows16 = lax.broadcasted_iota(jnp.int32, (16, 128), 0)
-
-    for step in (2, 1, 3, 0):
-        wanted = lax.rem(across + step, 4)
-        into = pack.at[step] if step else got.at[0]
-
-        def pack_tile(number, carry, wanted=wanted, into=into):
-            owner, tile = number // 4, number % 4
-
-            def held(d):
-                return table_s[wanted, owner, tile, d] & 63
-
-            into[owner, tile, 0:32, :] = every[held(first_dir), 1]
-            into[owner, tile, 32:64, :] = every[held(second_dir), 0]
-            corners = jnp.zeros((16, 128), F32)
-            for k, (d, which, at) in enumerate(((0, 1, 31), (2, 1, 0), (5, 0, 31), (7, 0, 0))):
-                near_rows = every[held(d), which, 16 * (at // 16) : 16 * (at // 16) + 16, :]
-                near_rows = near_rows.astype(F32)[at % 16 : at % 16 + 1]
-                corners = jnp.where(rows16 == k, near_rows, corners)
-            into[owner, tile, 64:80, :] = corners.astype(BF)
-            return carry
-
-        lax.fori_loop(0, 8, pack_tile, 0)
-        if step:
-            start(17 + step, pack.at[step], got.at[step], select_peer(step), 17 + step)
-    first_layer(3)
-    for step in range(1, 4):
-        arrived(17 + step, got.at[step])
-
-    def finish_tile(owner, tile):
-        def chosen(d, rows):
-            from_step = (across + 4 - (table_s[across, owner, tile, d] >> 6)) & 3
-            return got[from_step, owner, tile, rows, :]
-
-        piece[owner, tile, 0:32, :] = chosen(first_dir, slice(0, 32))
-        piece[owner, tile, 32:64, :] = chosen(second_dir, slice(32, 64))
-        corners = jnp.zeros((16, 128), F32)
-        for k, d in enumerate((0, 2, 5, 7)):
-            corners = jnp.where(rows16 == k, chosen(d, slice(64, 80)).astype(F32), corners)
-        piece[owner, tile, 64:80, :] = corners.astype(BF)
-
-    for owner, copies in (
-        (1 - core, ((23, ch_cross), (21, sibling))),
-        (core, ((22, ch_same),)),
-    ):
-        lax.fori_loop(0, 4, lambda tile, c, owner=owner: (finish_tile(owner, tile), c)[1], 0)
-        for number, peer in copies:
-            start(number, piece.at[owner], halo.at[core, ch], peer, number)
-    halo[core, ch] = piece[core]
-
     arrived(4, wm.at[1])
     arrived(5, wl_part.at[1])
     arrived(6, ws_part.at[1])
@@ -362,38 +311,120 @@
     blank = jnp.zeros((32, 128), BF)
     for line, lanes in ((32, 0), (33, 0), (0, 128), (33, 128), (0, 256), (1, 256)):
         mid_delta[line, :, lanes : lanes + 128] = blank
+    to_scalars.wait()
+    for far, plane in enumerate((zh, 1 - zh)):
+        arrived(ring_number(far, 1, 0), every.at[part(plane, before, 1)])
+        arrived(ring_number(far, 0, 1), every.at[part(plane, after, 0)])
+        arrived(14 + far * 2, every.at[part(plane, opposite, 0)])
+        arrived(15 + far * 2, every.at[part(plane, opposite, 1)])
+
+    first_dir = 1 + 2 * core
+    second_dir = 6 - 2 * core
+    rows16 = lax.broadcasted_iota(jnp.int32, (16, 128), 0)
+
+    got = (got_first, got_second)
+
+    def pack_round(step, turn):
+        wanted = lax.rem(across + step, 4)
+        into = pack.at[step, turn] if step else got[turn].at[0]
+
+        def pack_tile(slot, corners):
+            owner, tile = slot // 2, turn + 2 * (slot % 2)
+
+            def held(d):
+                return table_s[wanted, owner, tile, d] & 63
+
+            at = slot * 64
+            into[pl.ds(at, 32), :] = every[held(first_dir), 1]
+            into[pl.ds(at + 32, 32), :] = every[held(second_dir), 0]
+            for k, (d, which, line) in enumerate(CORNERS):
+                rows = every[held(d), which, 16 * (line // 16) : 16 * (line // 16) + 16, :]
+                row = rows.astype(F32)[line % 16 : line % 16 + 1]
+                corners = jnp.where(rows16 == slot * 4 + k, row, corners)
+            return corners
+
+        corners = jnp.zeros((16, 128), F32)
+        for slot in range(4):
+            corners = pack_tile(slot, corners)
+        into[256:272, :] = corners.astype(BF)
+        if step:
+            number = 17 + turn * 3 + step
+            start(number, pack.at[step, turn], got[turn].at[step], select_peer(step), number)
+
+    def finish_round(owner, turn):
+        def finish_tile(k, corners):
+            slot, tile = owner * 2 + k, turn + 2 * k
+
+            def chosen(d, rows):
+                from_step = (across + 4 - (table_s[across, owner, tile, d] >> 6)) & 3
+                return got[turn][from_step, rows, :]
+
+            at = pl.multiple_of(slot * 64, 64)
+            to = k * 64
+            piece[turn, owner, pl.ds(to, 32), :] = chosen(first_dir, pl.ds(at, 32))
+            piece[turn, owner, pl.ds(to + 32, 32), :] = chosen(second_dir, pl.ds(at + 32, 32))
+            for c, (d, _, _) in enumerate(CORNERS):
+                rows = chosen(d, slice(256, 272)).astype(F32)
+                corners = jnp.where(rows16 == slot * 4 + c, rows, corners)
+            return corners
+
+        corners = jnp.zeros((16, 128), F32)
+        for k in range(2):
+            corners = finish_tile(k, corners)
+        half = jnp.where(owner == 0, corners[0:8], corners[8:16])
+        both = jnp.concatenate([half, half], axis=0)
+        piece[turn, owner, 128:144, :] = both.astype(BF)
+
+    for turn in range(2):
+        for step in (2, 1, 3):
+            pack_round(step, turn)
+    pack_round(0, 0)
+    pack_round(0, 1)
+    first_layer(3)
+    for turn in range(2):
+        for step in range(1, 4):
+            arrived(17 + turn * 3 + step, got[turn].at[step])
+        for owner, copies in (
+            (1 - core, ((0, ch_cross), (1, sibling))),
+            (core, ((2, ch_same),)),
+        ):
+            finish_round(owner, turn)
+            for k, peer in copies:
+                number = 24 + turn * 3 + k
+                start(number, piece.at[turn, owner], halo.at[core, ch, turn], peer, number)
+        halo[core, ch, turn] = piece[turn, core]
+
+    def halo_arrived(turn):
+        arrived(24 + turn * 3, halo.at[1 - core, 1 - ch, turn])
+        arrived(25 + turn * 3, halo.at[1 - core, ch, turn])
+        arrived(26 + turn * 3, halo.at[core, 1 - ch, turn])
 
     loading[1].wait()
-    arrived(21, halo.at[1 - core, ch])
-    arrived(22, halo.at[core, 1 - ch])
-    arrived(23, halo.at[1 - core, 1 - ch])
 
 
     def here(tile, direction):
         return jnp.where(near_s[tile, direction] < 256, 1.0, 0.0).astype(F32)
 
-    def rim_features(tile):
+    def rim_features(turn, which):
+        rows = pl.ds(pl.multiple_of(which * 64, 64), 64)
+        parts = [(0, rows), (1, rows), (0, slice(128, 144))]
         return jnp.concatenate(
-            [
-                jnp.concatenate([halo[0, 0, tile], halo[0, 1, tile]], axis=1),
-                jnp.concatenate([halo[1, 0, tile], halo[1, 1, tile]], axis=1),
-            ],
+            [jnp.concatenate([halo[r, h, turn, at, :] for h in range(2)], axis=1) for r, at in parts],
             axis=0,
         )
 
-    def pad(tile):
-        pre = dot(rim_features(tile), w1[...]) + b1[...]
+    def pad(tile, turn, which):
+        pre = dot(rim_features(turn, which), w1[...]) + b1[...]
         rim_pre[...] = pre
         act = pre * sigmoid(pre)
         rim[...] = act
         padded[tile, 0, 8:40, :] = act[0:32] * here(tile, 1)
         padded[tile, 33, 8:40, :] = act[32:64] * here(tile, 6)
-        padded[tile, 1:33, 7:8, :] = (act[80:112] * here(tile, 3)).reshape(32, 1, 128)
-        padded[tile, 1:33, 40:41, :] = (act[112:144] * here(tile, 4)).reshape(32, 1, 128)
-        padded[tile, 0, 7:8, :] = rim[64:65, :] * here(tile, 0)
-        padded[tile, 0, 40:41, :] = rim[65:66, :] * here(tile, 2)
-        padded[tile, 33, 7:8, :] = rim[66:67, :] * here(tile, 5)
-        padded[tile, 33, 40:41, :] = rim[67:68, :] * here(tile, 7)
+        padded[tile, 1:33, 7:8, :] = (act[64:96] * here(tile, 3)).reshape(32, 1, 128)
+        padded[tile, 1:33, 40:41, :] = (act[96:128] * here(tile, 4)).reshape(32, 1, 128)
+        for k, (d, line, column) in enumerate(PLACES):
+            row = rim[pl.ds(128 + which * 4 + k, 1), :]
+            padded[tile, line, column : column + 1, :] = row * here(tile, d)
         for j in range(3):
             patches[:, :, j * 128 : j * 128 + 128] = padded[tile, :, 7 + j : 39 + j, :].astype(BF)
 
@@ -414,9 +445,6 @@
         out[tile, pl.ds(row, CHUNK), :] = val.astype(BF)
         return row, line, views, mid_sig, mid_val, mid_act, x_part, sig, val
 
-    def write_out(tile, number):
-        return pltpu.make_async_copy(out.at[tile], output.at[tile], out_sem.at[number])
-
     def forward_tile(tile, first, last):
         def body(number, carry):
             forward(tile, number)
@@ -426,7 +454,8 @@
 
     def whole_tile(k, carry):
         tile = 2 * ch + k
-        pad(tile)
+        halo_arrived(k)
+        pad(tile, k, ch)
 
         def body(number, inner):
             row, line, views, mid_sig, mid_val, mid_act, x_part, sig, val = forward(tile, number)
@@ -447,7 +476,6 @@
             return inner
 
         lax.fori_loop(0, 1024 // CHUNK, body, 0, unroll=True)
-        write_out(tile, k).start()
 
         back = dot(mid_delta[...].reshape(1088, 384), wbt[...]).reshape(34, 32, 384)
         spread[:, 0:8, :] = jnp.zeros((34, 8, 128), F32)
@@ -463,20 +491,19 @@
         rim[...] = jnp.zeros_like(rim)
         rim[0:32, :] = spread[0, 8:40, :] * here(tile, 1)
         rim[32:64, :] = spread[33, 8:40, :] * here(tile, 6)
-        rim[64:65, :] = spread[0, 7:8, :] * here(tile, 0)
-        rim[65:66, :] = spread[0, 40:41, :] * here(tile, 2)
-        rim[66:67, :] = spread[33, 7:8, :] * here(tile, 5)
-        rim[67:68, :] = spread[33, 40:41, :] * here(tile, 7)
-        rim[80:112, :] = spread[1:33, 7:8, :].reshape(32, 128) * here(tile, 3)
-        rim[112:144, :] = spread[1:33, 40:41, :].reshape(32, 128) * here(tile, 4)
+        rim[64:96, :] = spread[1:33, 7:8, :].reshape(32, 128) * here(tile, 3)
+        rim[96:128, :] = spread[1:33, 40:41, :].reshape(32, 128) * here(tile, 4)
+        for c, (d, line, column) in enumerate(PLACES):
+            row = spread[line, column : column + 1, :]
+            rim[pl.ds(128 + ch * 4 + c, 1), :] = row * here(tile, d)
         pre = rim_pre[...]
         sig = sigmoid(pre)
         slope = sig + pre * sig * (1.0 - sig)
         delta_rim = (rim[...] * slope).astype(BF)
         g_first[...] += dot_tn(delta, feat[tile].reshape(1024, 256))
-        g_first[...] += dot_tn(delta_rim, rim_features(tile))
+        g_first[...] += dot_tn(delta_rim, rim_features(k, ch))
         g_first_bias[...] += delta.astype(F32).reshape(128, 8, 128).sum(axis=0)
-        g_first_bias[...] += delta_rim.astype(F32).reshape(20, 8, 128).sum(axis=0)
+        g_first_bias[...] += delta_rim.astype(F32).reshape(18, 8, 128).sum(axis=0)
         return carry
 
     loading[13].wait()
@@ -537,7 +564,7 @@
     own_rows = pl.multiple_of(core * CORE_ROWS, CORE_ROWS)
     other_rows = pl.multiple_of((1 - core) * CORE_ROWS, CORE_ROWS)
     swap = hand(0, grads.at[:, pl.ds(other_rows, CORE_ROWS)], from_core, sibling)
-    pad(third)
+    pad(third, 0, 1 - ch)
     swap.wait_recv()
     for half in range(2):
         added = grads[half, pl.ds(own_rows, CORE_ROWS), :].astype(F32) + from_core[half].astype(F32)
@@ -547,7 +574,6 @@
         to = lax.rem(own_place + step, 16)
         plane.append(hand(step, by_piece.at[to], from_plane.at[step], plane_peer(step)))
     forward_tile(third, 0, count)
-    write_out(third, 2).start()
     added = by_piece[own_place].astype(F32)
     for step, made in enumerate(plane, 1):
         made.wait_recv()
@@ -556,7 +582,7 @@
     hops = []
     for k, (half, peer) in enumerate(((0, z_even), (1, ch_same), (1, z_odd))):
         hops.append(hand(16 + k, mine.at[half], from_z.at[k], peer))
-    pad(fourth)
+    pad(fourth, 1, 1 - ch)
     forward_tile(fourth, 0, count // 2)
     added = added[0]
     for k, made in enumerate(hops):
@@ -564,38 +590,28 @@
         added = added + from_z[k].astype(F32)
     at = pl.multiple_of(own_rows + own_place * PIECE, 16)
     done[pl.ds(at, PIECE), :] = added.astype(BF)
-    backs = []
+    def cross(step):
+        origin = lax.rem(own_place + 16 - step, 16)
+        rows = done.at[pl.ds(pl.multiple_of(own_rows + origin * PIECE, 16), PIECE)]
+        return hand(34 + step, rows, rows, sibling)
+
+    backs, crossings = [], []
     for step in range(1, 16):
         here_too = done.at[pl.ds(at, PIECE)]
         backs.append(hand(18 + step, here_too, here_too, plane_peer(step)))
+    crossings.append(cross(0))
     forward_tile(fourth, count // 2, count)
-    write_out(fourth, 3).start()
-    for made in backs:
+    for step, made in enumerate(backs, 1):
         made.wait_recv()
-    half_sum = done.at[pl.ds(own_rows, CORE_ROWS)]
-    last = hand(34, half_sum, half_sum, sibling)
-    last.wait_recv()
-    whole_sum = pltpu.make_async_copy(done, total, out_sem.at[4])
-    whole_sum.start()
+        crossings.append(cross(step))
+    for made in crossings:
+        made.wait_recv()
+    total[...] = done[...]
     for made in sent:
         made.wait_send()
-    for number, tile in enumerate((2 * ch, 2 * ch + 1, third, fourth)):
-        write_out(tile, number).wait()
-    whole_sum.wait()
-
-
-def block(
-    features,
-    cotangent,
-    neighbours,
-    w1,
-    b1,
-    wm,
-    mid_bias,
-    wl,
-    ws,
-    last_bias,
-):
+
+
+def block(*operands):
     scale = 1.0 / math.sqrt(4096)
     anywhere = pl.BlockSpec(memory_space=pl.ANY)
 
@@ -605,7 +621,7 @@
     return pl.pallas_call(
         kernel,
         in_specs=[anywhere] * 10,
-        out_specs=(anywhere, anywhere),
+        out_specs=(pl.BlockSpec(memory_space=pltpu.VMEM),) * 2,
         out_shape=(
             jax.ShapeDtypeStruct((4, 1024, 512), BF),
             jax.ShapeDtypeStruct((ROWS, 128), BF),
@@ -628,23 +644,23 @@
             pltpu.VMEM((8, 128), jnp.int32),
             pltpu.SMEM((4, 2, 8, 128), jnp.int32),
             pltpu.VMEM((64, 2, 32, 128), BF),
-            pltpu.VMEM((4, 2, 4, 80, 128), BF),
-            pltpu.VMEM((4, 2, 4, 80, 128), BF),
-            pltpu.VMEM((2, 4, 80, 128), BF),
-            pltpu.VMEM((2, 2, 4, 80, 128), BF),
+            pltpu.VMEM((4, 2, 272, 128), BF),
+            pltpu.VMEM((4, 272, 128), BF),
+            pltpu.VMEM((4, 272, 128), BF),
+            pltpu.VMEM((2, 2, 144, 128), BF),
+            pltpu.VMEM((2, 2, 2, 144, 128), BF),
             pltpu.VMEM((1, 128), F32),
             pltpu.VMEM((3, 384, 128), BF),
             pltpu.VMEM((384, 384), BF),
             pltpu.VMEM((128, 512), BF),
             pltpu.VMEM((256, 512), BF),
             pltpu.VMEM((4, 1024, 128), F32),
-            pltpu.VMEM((160, 128), F32),
+            pltpu.VMEM((144, 128), F32),
             pltpu.VMEM((4, 34, 48, 128), F32),
             pltpu.VMEM((34, 32, 384), BF),
             pltpu.VMEM((34, 32, 384), BF),
             pltpu.VMEM((34, 48, 128), F32),
-            pltpu.VMEM((160, 128), F32),
-            pltpu.VMEM((4, 1024, 512), BF),
+            pltpu.VMEM((144, 128), F32),
             pltpu.VMEM((128, 256), F32),
             pltpu.VMEM((3, 128, 384), F32),
             pltpu.VMEM((128, 512), F32),
@@ -660,21 +676,20 @@
             pltpu.VMEM((3, PIECE, 128), BF),
             pltpu.VMEM((ROWS, 128), BF),
             pltpu.SemaphoreType.DMA((16,)),
-            pltpu.SemaphoreType.DMA((5,)),
-            pltpu.SemaphoreType.DMA((24,)),
-            pltpu.SemaphoreType.DMA((24,)),
-            pltpu.SemaphoreType.DMA((35,)),
-            pltpu.SemaphoreType.DMA((35,)),
+            pltpu.SemaphoreType.DMA((38,)),
+            pltpu.SemaphoreType.DMA((38,)),
+            pltpu.SemaphoreType.DMA((50,)),
+            pltpu.SemaphoreType.DMA((50,)),
         ],
         compiler_params=pltpu.CompilerParams(
-            collective_id=0, has_side_effects=True, vmem_limit_bytes=60 * 2**20
+            collective_id=0, has_side_effects=True, vmem_limit_bytes=44 * 2**20
         ),
-    )(features, cotangent, neighbours, w1, b1, wm, mid_bias, wl, ws, last_bias)
+    )(*[pltpu.with_memory_space_constraint(a, pltpu.HBM) for a in operands])
 
 
 def finish_kernel(
     out,
-    total_h,
+    total,
     output,
     g_first,
     g_first_bias,
@@ -683,22 +698,11 @@
     g_last,
     g_side,
     g_last_bias,
-    total,
-    staged,
-    in_sem,
     out_sem,
 ):
-    loading = pltpu.make_async_copy(total_h, total, in_sem.at[PARTS])
-    loading.start()
-    reads, writes = [], []
-    for k in range(PARTS):
-        reads.append(pltpu.make_async_copy(out.at[k], staged.at[k], in_sem.at[k]))
-        writes.append(pltpu.make_async_copy(staged.at[k], output.at[k], out_sem.at[k]))
-        reads[k].start()
-    for k in range(PARTS):
-        reads[k].wait()
-        writes[k].start()
-    loading.wait()
+    writes = [pltpu.make_async_copy(out.at[k], output.at[k], out_sem.at[k]) for k in range(PARTS)]
+    for made in writes:
+        made.start()
 
     def rows(at, count):
         return total[at : at + count, :].astype(F32)
@@ -724,7 +728,7 @@
     vmem = pl.BlockSpec(memory_space=pltpu.VMEM)
     return pl.pallas_call(
         finish_kernel,
-        in_specs=[pl.BlockSpec(memory_space=pl.ANY)] * 2,
+        in_specs=[vmem, vmem],
         out_specs=(pl.BlockSpec(memory_space=pl.ANY), *[vmem] * 7),
         out_shape=(
             jax.ShapeDtypeStruct(out.shape, BF),
@@ -742,12 +746,9 @@
             ],
         ),
         scratch_shapes=[
-            pltpu.VMEM((ROWS, 128), BF),
-            pltpu.VMEM(out.shape, BF),
-            pltpu.SemaphoreType.DMA((PARTS + 1,)),
             pltpu.SemaphoreType.DMA((PARTS,)),
         ],
-        compiler_params=pltpu.CompilerParams(vmem_limit_bytes=60 * 2**20),
+        compiler_params=pltpu.CompilerParams(vmem_limit_bytes=16 * 2**20),
     )(out, total)
 
 

time: 67.7 us -> 62.1 us (0.917)
  Pallas kernels: 67 us -> 61.4 us
    pallas_call x2, Pallas kernels: 67 us -> 61.4 us  [the longest x1 58.4 us: block(): pl.pallas_call(kernel, in_specs=[anywhere] * 10, out_specs=(pl.BlockSpec(...]
where the time goes in v3:
time: 62.1 us; the launch traced here: 62 us
  Pallas kernels  61.4 us (99%)
  between operations  0.64 us (1%)
    pallas_call x1, Pallas kernels, block(): pl.pallas_call(kernel, in_specs=[anywhere] * 10, out_specs=(pl.BlockSpec(...  58.4 us
    pallas_call x1, Pallas kernels, finish(): pl.pallas_call(finish_kernel, in_specs=[vmem, vmem], out_specs=(pl.BlockS...  2.94 us

profile of v3, /device:TPU:1, one launch (start us, length us, event | category | flops | bytes accessed | tf_op | source)
XLA Modules:
  0.0 62.0 jit_solution(12035479027050197432)
XLA Ops:
  0.6 58.4 %shard_map.161 = (bf16[4,1024,512]{2,1,0:T(8,128)(2,1)S(1)}, bf16[1536,128]{1,0:T(8,128)(2,1)S(1)}) custom-call(bf16[4,32,32,256]{3,2,1,0:T(8,128)(2,1)} %refs_0_.1, bf16[4096,512]{1,0:T(8,128)(2,1)} %bitcast.15, s32[4,8]{1,0:T(4,128)} %refs_2_.1, bf16[256,128]{1,0:T(8,128)(2,1)} %refs_3_.1, f32[1,128]{1,0:T(1,128)} %bitcast.18, bf16[576,128]{1,0:T(8,128)(2,1)} %bitcast.16, ...), custom_call_target="tpu_custom_call" | custom-call | tf_op jit(solution)/shard_map/pallas_call | solution.py:621
  59.1 2.9 %shard_map.162 = (bf16[8,512,512]{2,1,0:T(8,128)(2,1)}, f32[64,256]{1,0:T(8,128)}, f32[1,64]{1,0:T(1,128)}, f32[3,3,64,128]{3,2,1,0:T(8,128)}, f32[1,64]{1,0:T(1...) custom-call(bf16[8,512,512]{2,1,0:T(8,128)(2,1)S(1)} %bitcast.14, ...), custom_call_target="tpu_custom_call" | custom-call | tf_op jit(solution)/shard_map/pallas_call | solution.py:729

commit v4 on v3

--- a/solution.py
+++ b/solution.py
@@ -24,6 +24,7 @@
 PLACES = ((0, 0, 7), (2, 0, 40), (5, 33, 7), (7, 33, 40))
 
 CHUNK = 512
+FAR_FIRST = (10, 6, 14, 9, 11, 5, 7, 13, 15, 2, 8, 1, 3, 4, 12)
 PARTS = 8
 
 
@@ -94,8 +95,9 @@
     wbt,
     wl,
     ws,
-    first_pre,
-    rim_pre,
+    first_slope,
+    feat_t,
+    rim_slope,
     padded,
     patches,
     mid_delta,
@@ -108,13 +110,13 @@
     g_first_bias,
     g_mid_bias,
     g_last_bias,
+    g_first_t,
     grads,
     from_core,
     by_piece,
     from_plane,
     mine,
     from_z,
-    done,
     local_sem,
     send_sem,
     recv_sem,
@@ -135,8 +137,14 @@
         to = lax.rem(across + step, 4)
         return device(jnp.where(row_role, to, y), zh, jnp.where(row_role, x, to), core, ch)
 
+    def plane_place(step, back=False):
+        rows, columns = step // 4, step % 4
+        if back:
+            rows, columns = 4 - rows, 4 - columns
+        return lax.rem(y + rows, 4) * 4 + lax.rem(x + columns, 4)
+
     def plane_peer(step):
-        to = lax.rem(own_place + step, 16)
+        to = plane_place(step)
         return device(to // 4, zh, to % 4, core, ch)
 
     sibling = device(y, zh, x, 1 - core, ch)
@@ -227,11 +235,16 @@
     def arrived(number, target):
         copy(0, target, target, sibling, number).wait_recv()
 
-    def first_layer(tile):
-        pre = dot(feat[tile].reshape(1024, 256), w1[...]) + b1[...]
-        first_pre[tile] = pre
-        act = pre * sigmoid(pre)
+    def first_layer(turn):
+        tile = lax.rem(2 * ch + turn, 4)
+        pixels = feat[tile].reshape(1024, 256)
+        pre = dot(pixels, w1[...]) + b1[...]
+        sig = sigmoid(pre)
+        act = pre * sig
         padded[tile, 1:33, 8:40, :] = act.reshape(32, 32, 128)
+        if turn < 2:
+            first_slope[turn] = sig + act * (1.0 - sig)
+            feat_t[turn] = pixels.T
 
     start(1, edges.at[1 - core, ch], every.at[part(zh, across, core)], sibling, 1)
     for k in range(2):
@@ -242,14 +255,11 @@
             z_peers[k],
             2 + core,
         )
-    def ring_number(far, owner, back):
-        return 30 + far * 4 + owner * 2 + back
-
     def ring(far, owner):
         strips = every.at[part(1 - zh if far else zh, along, owner)]
-        for back, peer in ((0, gather_peer(1)), (1, gather_peer(3))):
-            number = ring_number(far, owner, back)
-            start(number, strips, strips, peer, number)
+        first = 30 + (far * 2 + owner) * 3
+        for k in range(3):
+            start(first + k, strips, strips, gather_peer(k + 1), first + k)
 
     ring(0, core)
     start(0, table_out, table.at[along, core], sibling, 0)
@@ -272,14 +282,6 @@
     before = lax.rem(along + 3, 4)
     after = lax.rem(along + 1, 4)
     opposite = lax.rem(along + 2, 4)
-    for far, plane in enumerate((zh, 1 - zh)):
-        for owner, back, origin, peer in (
-            (0, 0, before, gather_peer(1)),
-            (1, 1, after, gather_peer(3)),
-        ):
-            passed = every.at[part(plane, origin, owner)]
-            arrived(ring_number(far, owner, back), passed)
-            start(14 + far * 2 + owner, passed, passed, peer, 14 + far * 2 + owner)
     for step in range(1, 4):
         arrived(8 + step, table.at[lax.rem(across + 4 - step, 4)])
     to_scalars = pltpu.make_async_copy(table, table_s, local_sem.at[len(loads)])
@@ -313,10 +315,10 @@
         mid_delta[line, :, lanes : lanes + 128] = blank
     to_scalars.wait()
     for far, plane in enumerate((zh, 1 - zh)):
-        arrived(ring_number(far, 1, 0), every.at[part(plane, before, 1)])
-        arrived(ring_number(far, 0, 1), every.at[part(plane, after, 0)])
-        arrived(14 + far * 2, every.at[part(plane, opposite, 0)])
-        arrived(15 + far * 2, every.at[part(plane, opposite, 1)])
+        for owner in range(2):
+            first = 30 + (far * 2 + owner) * 3
+            for k, origin in enumerate((before, opposite, after)):
+                arrived(first + k, every.at[part(plane, origin, owner)])
 
     first_dir = 1 + 2 * core
     second_dir = 6 - 2 * core
@@ -415,8 +417,9 @@
 
     def pad(tile, turn, which):
         pre = dot(rim_features(turn, which), w1[...]) + b1[...]
-        rim_pre[...] = pre
-        act = pre * sigmoid(pre)
+        sig = sigmoid(pre)
+        act = pre * sig
+        rim_slope[...] = sig + act * (1.0 - sig)
         rim[...] = act
         padded[tile, 0, 8:40, :] = act[0:32] * here(tile, 1)
         padded[tile, 33, 8:40, :] = act[32:64] * here(tile, 6)
@@ -462,7 +465,7 @@
             slope = sig + val * (1.0 - sig)
             grad_out = (cot[k, pl.ds(row, CHUNK), :].astype(F32) * scale * slope).astype(BF)
             g_last[...] += dot_tn(mid_act, grad_out)
-            g_side[...] += dot_tn(x_part, grad_out)
+            g_side[...] += dot(feat_t[k, :, pl.ds(row, CHUNK)], grad_out)
             g_last_bias[...] += grad_out.astype(F32).reshape(CHUNK // 8, 8, 512).sum(axis=0)
             mid_back = dot_nt(grad_out, wl[...])
             delta = (mid_back * (mid_sig + mid_val * (1.0 - mid_sig))).astype(BF)
@@ -484,10 +487,7 @@
         spread[:, 7:39, :] += back[:, :, 0:128]
         spread[:, 9:41, :] += back[:, :, 256:384]
 
-        pre = first_pre[tile]
-        sig = sigmoid(pre)
-        slope = sig + pre * sig * (1.0 - sig)
-        delta = (spread[1:33, 8:40, :].reshape(1024, 128) * slope).astype(BF)
+        delta = (spread[1:33, 8:40, :].reshape(1024, 128) * first_slope[k]).astype(BF)
         rim[...] = jnp.zeros_like(rim)
         rim[0:32, :] = spread[0, 8:40, :] * here(tile, 1)
         rim[32:64, :] = spread[33, 8:40, :] * here(tile, 6)
@@ -496,12 +496,8 @@
         for c, (d, line, column) in enumerate(PLACES):
             row = spread[line, column : column + 1, :]
             rim[pl.ds(128 + ch * 4 + c, 1), :] = row * here(tile, d)
-        pre = rim_pre[...]
-        sig = sigmoid(pre)
-        slope = sig + pre * sig * (1.0 - sig)
-        delta_rim = (rim[...] * slope).astype(BF)
-        g_first[...] += dot_tn(delta, feat[tile].reshape(1024, 256))
-        g_first[...] += dot_tn(delta_rim, rim_features(k, ch))
+        delta_rim = (rim[...] * rim_slope[...]).astype(BF)
+        g_first[...] += dot(feat_t[k], delta) + dot_tn(rim_features(k, ch), delta_rim)
         g_first_bias[...] += delta.astype(F32).reshape(128, 8, 128).sum(axis=0)
         g_first_bias[...] += delta_rim.astype(F32).reshape(18, 8, 128).sum(axis=0)
         return carry
@@ -511,6 +507,7 @@
     lax.fori_loop(0, 2, whole_tile, 0)
 
 
+    g_first_t[...] = g_first[...].T
     bias_first = jnp.sum(g_first_bias[...], axis=0, keepdims=True)
     bias_mid = jnp.sum(g_mid_bias[...], axis=0, keepdims=True)
     bias_last = jnp.sum(g_last_bias[...], axis=0, keepdims=True)
@@ -522,7 +519,7 @@
         for k in range(2):
             at = ROW_FIRST + k * 64
             lanes = slice(k * 128, k * 128 + 128)
-            grads[half, at : at + 64, :] = g_first[pl.ds(start64, 64), lanes].astype(BF)
+            grads[half, at : at + 64, :] = g_first_t[pl.ds(start64, 64), lanes].astype(BF)
         for i in range(3):
             for j in range(3):
                 at = ROW_MID + (i * 3 + j) * 64
@@ -570,12 +567,12 @@
         added = grads[half, pl.ds(own_rows, CORE_ROWS), :].astype(F32) + from_core[half].astype(F32)
         by_piece[:, half] = added.astype(BF).reshape(16, PIECE, 128)
     plane = []
-    for step in range(1, 16):
-        to = lax.rem(own_place + step, 16)
-        plane.append(hand(step, by_piece.at[to], from_plane.at[step], plane_peer(step)))
+    for step in FAR_FIRST:
+        piece_of = by_piece.at[plane_place(step)]
+        plane.append((step, hand(step, piece_of, from_plane.at[step], plane_peer(step))))
     forward_tile(third, 0, count)
     added = by_piece[own_place].astype(F32)
-    for step, made in enumerate(plane, 1):
+    for step, made in reversed(plane):
         made.wait_recv()
         added = added + from_plane[step].astype(F32)
     mine[...] = added.astype(BF)
@@ -589,24 +586,23 @@
         made.wait_recv()
         added = added + from_z[k].astype(F32)
     at = pl.multiple_of(own_rows + own_place * PIECE, 16)
-    done[pl.ds(at, PIECE), :] = added.astype(BF)
+    total[pl.ds(at, PIECE), :] = added.astype(BF)
     def cross(step):
-        origin = lax.rem(own_place + 16 - step, 16)
-        rows = done.at[pl.ds(pl.multiple_of(own_rows + origin * PIECE, 16), PIECE)]
+        origin = plane_place(step, back=True)
+        rows = total.at[pl.ds(pl.multiple_of(own_rows + origin * PIECE, 16), PIECE)]
         return hand(34 + step, rows, rows, sibling)
 
     backs, crossings = [], []
-    for step in range(1, 16):
-        here_too = done.at[pl.ds(at, PIECE)]
-        backs.append(hand(18 + step, here_too, here_too, plane_peer(step)))
+    for step in FAR_FIRST:
+        here_too = total.at[pl.ds(at, PIECE)]
+        backs.append((step, hand(18 + step, here_too, here_too, plane_peer(step))))
     crossings.append(cross(0))
     forward_tile(fourth, count // 2, count)
-    for step, made in enumerate(backs, 1):
+    for step, made in reversed(backs):
         made.wait_recv()
         crossings.append(cross(step))
     for made in crossings:
         made.wait_recv()
-    total[...] = done[...]
     for made in sent:
         made.wait_send()
 
@@ -654,30 +650,31 @@
             pltpu.VMEM((384, 384), BF),
             pltpu.VMEM((128, 512), BF),
             pltpu.VMEM((256, 512), BF),
-            pltpu.VMEM((4, 1024, 128), F32),
+            pltpu.VMEM((2, 1024, 128), F32),
+            pltpu.VMEM((2, 256, 1024), BF),
             pltpu.VMEM((144, 128), F32),
             pltpu.VMEM((4, 34, 48, 128), F32),
             pltpu.VMEM((34, 32, 384), BF),
             pltpu.VMEM((34, 32, 384), BF),
             pltpu.VMEM((34, 48, 128), F32),
             pltpu.VMEM((144, 128), F32),
-            pltpu.VMEM((128, 256), F32),
+            pltpu.VMEM((256, 128), F32),
             pltpu.VMEM((3, 128, 384), F32),
             pltpu.VMEM((128, 512), F32),
             pltpu.VMEM((256, 512), F32),
             pltpu.VMEM((8, 128), F32),
             pltpu.VMEM((8, 128), F32),
             pltpu.VMEM((8, 512), F32),
+            pltpu.VMEM((128, 256), F32),
             pltpu.VMEM((2, ROWS, 128), BF),
             pltpu.VMEM((2, CORE_ROWS, 128), BF),
             pltpu.VMEM((16, 2, PIECE, 128), BF),
             pltpu.VMEM((16, 2, PIECE, 128), BF),
             pltpu.VMEM((2, PIECE, 128), BF),
             pltpu.VMEM((3, PIECE, 128), BF),
-            pltpu.VMEM((ROWS, 128), BF),
             pltpu.SemaphoreType.DMA((16,)),
-            pltpu.SemaphoreType.DMA((38,)),
-            pltpu.SemaphoreType.DMA((38,)),
+            pltpu.SemaphoreType.DMA((42,)),
+            pltpu.SemaphoreType.DMA((42,)),
             pltpu.SemaphoreType.DMA((50,)),
             pltpu.SemaphoreType.DMA((50,)),
         ],
@@ -698,24 +695,39 @@
     g_last,
     g_side,
     g_last_bias,
+    first_v,
+    mid_v,
+    last_v,
+    side_v,
     out_sem,
 ):
     writes = [pltpu.make_async_copy(out.at[k], output.at[k], out_sem.at[k]) for k in range(PARTS)]
     for made in writes:
         made.start()
 
+    def send(number, source, target):
+        made = pltpu.make_async_copy(source, target, out_sem.at[PARTS + number])
+        made.start()
+        writes.append(made)
+
     def rows(at, count):
         return total[at : at + count, :].astype(F32)
 
+    for k in range(4):
+        lanes = slice(k * 128, k * 128 + 128)
+        side_v[:, lanes] = rows(ROW_SIDE + k * 128, 128)
+        last_v[:, lanes] = rows(ROW_LAST + k * 64, 64)
+    send(0, side_v, g_side)
+    send(1, last_v, g_last)
+    for k in range(9):
+        mid_v[k // 3, k % 3] = rows(ROW_MID + k * 64, 64)
+    send(2, mid_v, g_mid)
     for k in range(2):
-        g_first[:, k * 128 : k * 128 + 128] = rows(ROW_FIRST + k * 64, 64)
-    for k in range(9):
-        g_mid[k // 3, k % 3] = rows(ROW_MID + k * 64, 64)
+        first_v[:, k * 128 : k * 128 + 128] = rows(ROW_FIRST + k * 64, 64)
+    send(3, first_v, g_first)
     bias = rows(ROW_BIAS, 16)
     for k in range(4):
         lanes = slice(k * 128, k * 128 + 128)
-        g_last[:, lanes] = rows(ROW_LAST + k * 64, 64)
-        g_side[:, lanes] = rows(ROW_SIDE + k * 128, 128)
         g_last_bias[:, lanes] = bias[2 + k : 3 + k, :]
     ch = lax.axis_index("ch")
     g_first_bias[...] = jnp.where(ch == 0, bias[0:1, 0:64], bias[0:1, 64:128])
@@ -726,10 +738,11 @@
 
 def finish(out, total):
     vmem = pl.BlockSpec(memory_space=pltpu.VMEM)
+    anywhere = pl.BlockSpec(memory_space=pl.ANY)
     return pl.pallas_call(
         finish_kernel,
         in_specs=[vmem, vmem],
-        out_specs=(pl.BlockSpec(memory_space=pl.ANY), *[vmem] * 7),
+        out_specs=(anywhere, anywhere, vmem, anywhere, vmem, anywhere, anywhere, vmem),
         out_shape=(
             jax.ShapeDtypeStruct(out.shape, BF),
             *[
@@ -746,7 +759,11 @@
             ],
         ),
         scratch_shapes=[
-            pltpu.SemaphoreType.DMA((PARTS,)),
+            pltpu.VMEM((64, 256), F32),
+            pltpu.VMEM((3, 3, 64, 128), F32),
+            pltpu.VMEM((64, 512), F32),
+            pltpu.VMEM((128, 512), F32),
+            pltpu.SemaphoreType.DMA((PARTS + 4,)),
         ],
         compiler_params=pltpu.CompilerParams(vmem_limit_bytes=16 * 2**20),
     )(out, total)

time: 62.1 us -> 60.9 us (0.981)
  Pallas kernels: 61.4 us -> 60 us
    pallas_call x1, Pallas kernels: 58.4 us -> 57.1 us  [block(): pl.pallas_call(kernel, in_specs=[anywhere] * 10, out_specs=(pl.BlockSpec(...]
where the time goes in v4:
time: 60.9 us; the launch traced here: 60.8 us
  Pallas kernels  60 us (99%)
  between operations  0.81 us (1%)
    pallas_call x1, Pallas kernels, block(): pl.pallas_call(kernel, in_specs=[anywhere] * 10, out_specs=(pl.BlockSpec(...  57.1 us
    pallas_call x1, Pallas kernels, finish(): pl.pallas_call(finish_kernel, in_specs=[vmem, vmem], out_specs=(anywhere,...  2.91 us

profile of v4, /device:TPU:1, one launch (start us, length us, event | category | flops | bytes accessed | tf_op | source)
XLA Modules:
  0.0 60.8 jit_solution(2053496765295758388)
XLA Ops:
  0.6 57.1 %shard_map.161 = (bf16[4,1024,512]{2,1,0:T(8,128)(2,1)S(1)}, bf16[1536,128]{1,0:T(8,128)(2,1)S(1)}) custom-call(bf16[4,32,32,256]{3,2,1,0:T(8,128)(2,1)} %refs_0_.1, bf16[4096,512]{1,0:T(8,128)(2,1)} %bitcast.15, s32[4,8]{1,0:T(4,128)} %refs_2_.1, bf16[256,128]{1,0:T(8,128)(2,1)} %refs_3_.1, f32[1,128]{1,0:T(1,128)} %bitcast.18, bf16[576,128]{1,0:T(8,128)(2,1)} %bitcast.16, ...), custom_call_target="tpu_custom_call" | custom-call | tf_op jit(solution)/shard_map/pallas_call | solution.py:617
  57.8 2.9 %shard_map.162 = (bf16[8,512,512]{2,1,0:T(8,128)(2,1)}, f32[64,256]{1,0:T(8,128)}, f32[1,64]{1,0:T(1,128)}, f32[3,3,64,128]{3,2,1,0:T(8,128)}, f32[1,64]{1,0:T(1...) custom-call(bf16[8,512,512]{2,1,0:T(8,128)(2,1)S(1)} %bitcast.14, ...), custom_call_target="tpu_custom_call" | custom-call | tf_op jit(solution)/shard_map/pallas_call | solution.py:742

commit v5 on v4

--- a/solution.py
+++ b/solution.py
@@ -179,7 +179,8 @@
     loading = []
     for number, (source, target) in enumerate(loads):
         made = pltpu.make_async_copy(source, target, local_sem.at[number])
-        made.start()
+        if number < 13:
+            made.start()
         loading.append(made)
 
     loading[0].wait()
@@ -199,12 +200,14 @@
         last_row = feat[tile, 31]
         for half in range(2):
             lanes = slice(half * 128, half * 128 + 128)
-            wide[0:512, :] = feat[tile, :, 0:16, lanes].astype(F32).reshape(512, 128)
-            wide[512:1024, :] = feat[tile, :, 16:32, lanes].astype(F32).reshape(512, 128)
+            low_columns = feat[tile, :, 0:16, lanes].astype(F32)[:, 0:8]
+            high_columns = feat[tile, :, 16:32, lanes].astype(F32)[:, 8:16]
+            wide[0:256, :] = low_columns.reshape(256, 128)
+            wide[256:512, :] = high_columns.reshape(256, 128)
             edges[0, half, tile, 0] = first_row[:, lanes]
             edges[0, half, tile, 1] = last_row[:, lanes]
-            edges[1, half, tile, 0] = wide[pl.ds(0, 32, stride=16), :].astype(BF)
-            edges[1, half, tile, 1] = wide[pl.ds(527, 32, stride=16), :].astype(BF)
+            edges[1, half, tile, 0] = wide[pl.ds(0, 32, stride=8), :].astype(BF)
+            edges[1, half, tile, 1] = wide[pl.ds(263, 32, stride=8), :].astype(BF)
 
     def part(plane, at, owner):
         return pl.ds(pl.multiple_of(plane * 32 + at * 8 + owner * 4, 4), 4)
@@ -266,6 +269,8 @@
     start(4, wm.at[0], wm.at[1], ch_same, 4)
     start(5, wl_part.at[0], wl_part.at[1], ch_same, 5)
     start(6, ws_part.at[0], ws_part.at[1], ch_same, 6)
+    loading[13].start()
+    loading[14].start()
     loading[6].wait()
     loading[7].wait()
     first_layer(0)
@@ -634,7 +639,7 @@
             pltpu.VMEM((2, 64, 512), BF),
             pltpu.VMEM((2, 128, 512), BF),
             pltpu.VMEM((1, 512), F32),
-            pltpu.VMEM((1024, 128), F32),
+            pltpu.VMEM((512, 128), F32),
             pltpu.VMEM((2, 2, 4, 2, 32, 128), BF),
             pltpu.VMEM((4, 2, 8, 128), jnp.int32),
             pltpu.VMEM((8, 128), jnp.int32),

time: 60.9 us -> 61 us (level)
  no operation moved by 1% of the time
where the time goes in v5:
time: 61 us; the launch traced here: 60.8 us
  Pallas kernels  60 us (98%)
  between operations  0.81 us (1%)
    pallas_call x1, Pallas kernels, block(): pl.pallas_call(kernel, in_specs=[anywhere] * 10, out_specs=(pl.BlockSpec(...  57.1 us
    pallas_call x1, Pallas kernels, finish(): pl.pallas_call(finish_kernel, in_specs=[vmem, vmem], out_specs=(anywhere,...  2.91 us

profile of v5, /device:TPU:1, one launch (start us, length us, event | category | flops | bytes accessed | tf_op | source)
XLA Modules:
  0.0 60.8 jit_solution(13751783414129512559)
XLA Ops:
  0.6 57.1 %shard_map.161 = (bf16[4,1024,512]{2,1,0:T(8,128)(2,1)S(1)}, bf16[1536,128]{1,0:T(8,128)(2,1)S(1)}) custom-call(bf16[4,32,32,256]{3,2,1,0:T(8,128)(2,1)} %refs_0_.1, bf16[4096,512]{1,0:T(8,128)(2,1)} %bitcast.15, s32[4,8]{1,0:T(4,128)} %refs_2_.1, bf16[256,128]{1,0:T(8,128)(2,1)} %refs_3_.1, f32[1,128]{1,0:T(1,128)} %bitcast.18, bf16[576,128]{1,0:T(8,128)(2,1)} %bitcast.16, ...), custom_call_target="tpu_custom_call" | custom-call | tf_op jit(solution)/shard_map/pallas_call | solution.py:622
  57.8 2.9 %shard_map.162 = (bf16[8,512,512]{2,1,0:T(8,128)(2,1)}, f32[64,256]{1,0:T(8,128)}, f32[1,64]{1,0:T(1,128)}, f32[3,3,64,128]{3,2,1,0:T(8,128)}, f32[1,64]{1,0:T(1...) custom-call(bf16[8,512,512]{2,1,0:T(8,128)(2,1)S(1)} %bitcast.14, ...), custom_call_target="tpu_custom_call" | custom-call | tf_op jit(solution)/shard_map/pallas_call | solution.py:747
